TPU v7x, 256 devices: a whole 4x4x8 slice. The times are simulated.
256 devices in a mesh: dcn: 4 (over x), fsdp: 16 (over y, z_lo), tp: 4 (over z_hi, core).
Axes of the slice: x: 4, y: 4, z: 8 (z_hi: 2, z_lo: 4; z = z_hi * 4 + z_lo), core: 2. Of those that a mesh axis runs over, the one named last changes fastest.
Arguments:
- inputs: bfloat16 [320, 4608], P(None, 'dcn'), may hold values from -6 to 6
- target: bfloat16 [320, 4608], P(None, 'dcn'), may hold values from -6 to 6
- w_gate: bfloat16 [4608, 18432], P(('dcn', 'fsdp'), 'tp'), may hold values from -0.09375 to 0.09375
- w_up: bfloat16 [4608, 18432], P(('dcn', 'fsdp'), 'tp'), may hold values from -0.09375 to 0.09375
- w_down: bfloat16 [18432, 4608], P('tp', ('dcn', 'fsdp')), may hold values from -0.046875 to 0.046875
- start_gate: bfloat16 [4608, 18432], P(('dcn', 'fsdp'), 'tp'), may hold values from -350 to 350
- start_up: bfloat16 [4608, 18432], P(('dcn', 'fsdp'), 'tp'), may hold values from -350 to 350
- start_down: bfloat16 [18432, 4608], P('tp', ('dcn', 'fsdp')), may hold values from -350 to 350
Outputs:
- next_gate: float32 [4608, 4, 4608], P('dcn', 'tp', 'fsdp')
- next_up: float32 [4608, 4, 4608], P('dcn', 'tp', 'fsdp')
- next_down: float32 [4, 4608, 4608], P('tp', 'fsdp', 'dcn')
- hessenberg: float32 [4], replicated
- rayleigh: float32 [1], replicated
All inputs are finite; a program needn't handle non-finite values.
Results may differ from a plain program's by a relative error of at most 0.014.
Values may be sent and summed in bfloat16 or wider, within the bound.
A program may use at most 64 MiB of HBM per device.

v0:
```python
import math

import jax
import jax.numpy as jnp
from jax import lax
from jax.sharding import PartitionSpec as P

D = 4608
FF = 18432


gelu_cubic = 0.044715
gelu_scale = math.sqrt(2.0 / math.pi)
epsilon = 1e-06


def gelu_parts(argument):
    squared = argument * argument
    inner_arg = gelu_scale * (argument + gelu_cubic * squared * argument)
    tanh_val = jnp.tanh(inner_arg)
    sech_square = 1.0 - tanh_val * tanh_val
    inner_slope = gelu_scale * (1.0 + 3.0 * gelu_cubic * squared)
    inner_curve = gelu_scale * 6.0 * gelu_cubic * argument
    gelu_val = 0.5 * argument * (1.0 + tanh_val)
    gelu_slope = 0.5 * (1.0 + tanh_val) + 0.5 * argument * sech_square * inner_slope
    gelu_curve = sech_square * inner_slope + 0.5 * argument * (
        sech_square * inner_curve - 2.0 * tanh_val * sech_square * inner_slope * inner_slope
    )
    return (gelu_val, gelu_slope, gelu_curve)


def product(former, latter):
    return jnp.dot(former, latter, preferred_element_type=jnp.float32)


def contract_last(former, latter):
    return lax.dot_general(
        former, latter, (((1,), (1,)), ((), ())), preferred_element_type=jnp.float32
    )


def contract_first(former, latter):
    return lax.dot_general(
        former, latter, (((0,), (0,)), ((), ())), preferred_element_type=jnp.float32
    )


def local_dot(former, latter):
    return (
        jnp.sum(former[0] * latter[0])
        + jnp.sum(former[1] * latter[1])
        + jnp.sum(former[2] * latter[2])
    )


def feature_sum(former, latter):
    return lax.psum((former, latter), "dcn")


def back_sum(partial_grad):
    return lax.psum(partial_grad, "dcn")


def projections(values):
    return lax.psum((values[0], values[1]), ("dcn", "fsdp", "tp"))


def residual_norm(value):
    return lax.psum(value, ("dcn", "fsdp", "tp"))


def out_grad(partial_out, aimed, count_tok):
    whole = lax.psum(partial_out, ("fsdp", "tp"))
    if aimed is not None:
        whole = whole - aimed.astype(jnp.float32)
    return (whole / count_tok).astype(jnp.bfloat16)


def on_device(inputs, target, w_gate, w_up, w_down, start_gate, start_up, start_down):
    gate_cols, up_cols, start_gcols, start_ucols = (
        lax.all_to_all(w_gate, "fsdp", split_axis=1, concat_axis=0, tiled=True),
        lax.all_to_all(w_up, "fsdp", split_axis=1, concat_axis=0, tiled=True),
        lax.all_to_all(start_gate, "fsdp", split_axis=1, concat_axis=0, tiled=True),
        lax.all_to_all(start_up, "fsdp", split_axis=1, concat_axis=0, tiled=True),
    )
    down_rows, start_drows = (
        lax.all_to_all(w_down, "fsdp", split_axis=0, concat_axis=1, tiled=True),
        lax.all_to_all(start_down, "fsdp", split_axis=0, concat_axis=1, tiled=True),
    )
    count_tok = inputs.shape[0]
    entries = jnp.float32(3 * D * FF)
    gate_pre, up_pre = feature_sum(product(inputs, gate_cols), product(inputs, up_cols))
    gelu_val, gelu_slope, gelu_curve = gelu_parts(gate_pre)
    hidden = (gelu_val * up_pre).astype(jnp.bfloat16)
    grad_out = out_grad(product(hidden, down_rows), target, count_tok)
    grad_hidden = back_sum(contract_last(grad_out, down_rows))

    def hessian_apply(vector):
        tan_gate = vector[0].astype(jnp.bfloat16)
        tan_up = vector[1].astype(jnp.bfloat16)
        tan_down = vector[2].astype(jnp.bfloat16)
        gate_dot, up_dot = feature_sum(product(inputs, tan_gate), product(inputs, tan_up))
        hidden_dot = (gelu_slope * gate_dot * up_pre + gelu_val * up_dot).astype(jnp.bfloat16)
        grad_dot = out_grad(
            product(hidden_dot, down_rows) + product(hidden, tan_down), None, count_tok
        )
        back_dot = back_sum(contract_last(grad_dot, down_rows) + contract_last(grad_out, tan_down))
        gate_term = (
            back_dot * up_pre * gelu_slope
            + grad_hidden * up_dot * gelu_slope
            + grad_hidden * up_pre * gelu_curve * gate_dot
        ).astype(jnp.bfloat16)
        up_term = (back_dot * gelu_val + grad_hidden * gelu_slope * gate_dot).astype(jnp.bfloat16)
        return (
            contract_first(inputs, gate_term),
            contract_first(inputs, up_term),
            contract_first(hidden_dot, grad_out) + contract_first(hidden, grad_dot),
        )

    start_vec = (
        start_gcols.astype(jnp.float32),
        start_ucols.astype(jnp.float32),
        start_drows.astype(jnp.float32),
    )
    image_one = hessian_apply(start_vec)
    self_sq, cross = projections((local_dot(start_vec, start_vec), local_dot(start_vec, image_one)))
    norm_sq = self_sq / entries
    factor = 1.0 / jnp.sqrt(norm_sq + epsilon)
    arnoldi_11 = cross / entries * factor * factor
    basis_one = tuple((member * factor for member in start_vec))
    applied = tuple((member * factor for member in image_one))
    residual = tuple((later - arnoldi_11 * earlier for later, earlier in zip(applied, basis_one)))
    resid_sq = residual_norm(local_dot(residual, residual)) / entries
    arnoldi_21 = jnp.sqrt(resid_sq + epsilon)
    basis_two = tuple((member / arnoldi_21 for member in residual))
    image_two = hessian_apply(basis_two)
    first_sum, second_sum = projections(
        (local_dot(basis_one, image_two), local_dot(basis_two, image_two))
    )
    arnoldi_12 = first_sum / entries
    arnoldi_22 = second_sum / entries
    residual = tuple(
        (
            later - arnoldi_12 * first_vec - arnoldi_22 * second_vec
            for later, first_vec, second_vec in zip(image_two, basis_one, basis_two)
        )
    )
    resid_sq = residual_norm(local_dot(residual, residual)) / entries
    arnoldi_32 = jnp.sqrt(resid_sq + epsilon)
    basis_three = tuple((member / arnoldi_32 for member in residual))
    next_gate = basis_three[0].reshape(basis_three[0].shape[0], 1, basis_three[0].shape[1])
    next_up = basis_three[1].reshape(basis_three[1].shape[0], 1, basis_three[1].shape[1])
    next_down = basis_three[2].reshape(1, basis_three[2].shape[0], basis_three[2].shape[1])
    hessenberg = jnp.stack([arnoldi_21, arnoldi_12, arnoldi_22, arnoldi_32])
    rayleigh = jnp.stack([arnoldi_11])
    return (next_gate, next_up, next_down, hessenberg, rayleigh)


def solution(mesh):
    placed = (
        P(None, "dcn"),
        P(None, "dcn"),
        P(("dcn", "fsdp"), "tp"),
        P(("dcn", "fsdp"), "tp"),
        P("tp", ("dcn", "fsdp")),
        P(("dcn", "fsdp"), "tp"),
        P(("dcn", "fsdp"), "tp"),
        P("tp", ("dcn", "fsdp")),
    )
    return jax.shard_map(
        on_device,
        mesh=mesh,
        in_specs=placed,
        out_specs=(
            P("dcn", "tp", "fsdp"),
            P("dcn", "tp", "fsdp"),
            P("tp", "fsdp", "dcn"),
            P(),
            P(),
        ),
        check_vma=False,
    )
```

profile of v0, /device:TPU:1, one launch (start us, length us, event | category | flops | bytes accessed | tf_op | source)
XLA Modules:
  0.0 1096.8 jit_solution(12106337068764381488)
XLA Ops:
  10.7 9.3 all-to-all-start.1
  22.4 21.2 %all-to-all-done.1 = bf16[72,16,288]{2,0,1:T(8,128)(2,1)S(1)} async-done(((bf16[72,16,288]{2,0,1:T(8,128)(2,1)}), bf16[72,16,288]{2,0,1:T(8,128)(2,1)S(1)}, u32[]{:S(2)}, u32[]{:S(2)}) %all-to-all-start.1) | async-done | bytes 663584 | tf_op jit(solution)/shard_map/all_to_all | solution.py:83
  43.5 4.2 all-to-all-start.2
  51.2 20.0 %all-to-all-done.2 = bf16[72,16,288]{2,0,1:T(8,128)(2,1)S(1)} async-done(((bf16[72,16,288]{2,0,1:T(8,128)(2,1)}), bf16[72,16,288]{2,0,1:T(8,128)(2,1)S(1)}, u32[]{:S(2)}, u32[]{:S(2)}) %all-to-all-start.2) | async-done | bytes 663584 | tf_op jit(solution)/shard_map/all_to_all | solution.py:82
  71.2 4.3 all-to-all-start
  79.0 20.0 %all-to-all-done = bf16[72,16,288]{2,0,1:T(8,128)(2,1)} async-done(((bf16[72,16,288]{2,0,1:T(8,128)(2,1)}), bf16[72,16,288]{2,0,1:T(8,128)(2,1)}, u32[]{:S(2)}, u32[]{:S(2)}) %all-to-all-start) | async-done | bytes 663584 | tf_op jit(solution)/shard_map/all_to_all | solution.py:81
  98.9 3.7 all-to-all-start.3
  108.9 2.5 fusion.82
  111.4 14.7 %all-to-all-done.3 = bf16[72,16,288]{2,0,1:T(8,128)(2,1)S(1)} async-done(((bf16[72,16,288]{2,0,1:T(8,128)(2,1)}), bf16[72,16,288]{2,0,1:T(8,128)(2,1)S(1)}, u32[]{:S(2)}, u32[]{:S(2)}) %all-to-all-start.3) | async-done | bytes 663584 | tf_op jit(solution)/shard_map/all_to_all | solution.py:84
  126.1 3.9 all-to-all-start.4
  135.4 18.0 %all-to-all-done.4 = bf16[16,288,72]{1,2,0:T(8,128)(2,1)S(1)} async-done(((bf16[16,288,72]{1,2,0:T(8,128)(2,1)}), bf16[16,288,72]{1,2,0:T(8,128)(2,1)S(1)}, u32[]{:S(2)}, u32[]{:S(2)}) %all-to-all-start.4) | async-done | bytes 663584 | tf_op jit(solution)/shard_map/all_to_all | solution.py:87
  153.4 4.3 all-to-all-start.5
  157.8 35.9 %all-reduce.23.cloned.1.call-done = (f32[320,288]{0,1:T(8,128)}, f32[320,288]{0,1:T(8,128)}, f32[320,288]{0,1:T(8,128)}, f32[320,288]{0,1:T(8,128)}) async-done(((f32[320,288]{0,1:T(8,128)}, f32[320,288]{0,1:T(8,128)}, f32[320,288]{0,1:T(8,128)}, f32[320,288]{0,1:T(8,128)}), (f32[320,288]{0,1:T(8,128)}, f32[320,288]{0,1:T(8,128)}, f32[320,288]{0,1:T(8,128)}, ...) | async-done | bytes 1474576 | tf_op jit(solution)/shard_map/psum | solution.py:57
  199.0 3.3 convolution_add_fusion.1
  210.5 182.3 %all-reduce.17.cloned.1.call-done = (f32[320,1152]{1,0:T(8,128)}, f32[320,1152]{1,0:T(8,128)}) async-done(((f32[320,1152]{1,0:T(8,128)}, f32[320,1152]{1,0:T(8,128)}), (f32[320,1152]{1,0:T(8,128)}, f32[320,1152]{1,0:T(8,128)})) %all-reduce.17.cloned.1.call-update) | async-done | bytes 2949136 | tf_op jit(solution)/shard_map/psum | solution.py:73
  404.0 43.3 %all-reduce.21.cloned.1.call-done = (f32[320,288]{0,1:T(8,128)}, f32[320,288]{0,1:T(8,128)}) async-done(((f32[320,288]{0,1:T(8,128)}, f32[320,288]{0,1:T(8,128)}), (f32[320,288]{0,1:T(8,128)}, f32[320,288]{0,1:T(8,128)})) %all-reduce.21.cloned.1.call-update) | async-done | bytes 737296 | tf_op jit(solution)/shard_map/psum | solution.py:61
  447.4 4.5 fusion.13
  456.2 77.7 %all-reduce.1 = (f32[]{:T(128)}, f32[]{:T(128)}) all-reduce(f32[]{:T(128)S(6)} %add.155, f32[]{:T(128)S(6)} %add.150), channel_id=1, replica_groups=mesh['dcn'=4,'fsdp'=16,'tp'=4] {'dcn','fsdp','tp'}, use_global_device_ids=true, to_apply=%region_15.0 | all-reduce | flops 2 | bytes 16 | tf_op jit(solution)/shard_map/psum | solution.py:65
  535.3 2.6 multiply_reduce_fusion.11
  541.8 73.5 %psum.136 = f32[]{:T(128)} all-reduce(f32[]{:T(128)S(6)} %add.157), channel_id=1, replica_groups=mesh['dcn'=4,'fsdp'=16,'tp'=4] {'dcn','fsdp','tp'}, use_global_device_ids=true, to_apply=%region_19.0 | all-reduce | flops 1 | bytes 8 | tf_op jit(solution)/shard_map/psum | solution.py:69
  616.0 3.0 convolution_bitcast_fusion.5
  620.4 45.0 %all-reduce.19.cloned.1.call-done = (f32[320,288]{0,1:T(8,128)}, f32[320,288]{0,1:T(8,128)}) async-done(((f32[320,288]{0,1:T(8,128)}, f32[320,288]{0,1:T(8,128)}), (f32[320,288]{0,1:T(8,128)}, f32[320,288]{0,1:T(8,128)})) %all-reduce.19.cloned.1.call-update) | async-done | bytes 737296 | tf_op jit(solution)/shard_map/psum | solution.py:57
  670.7 2.8 fusion.91
  673.6 186.0 %all-reduce.13.cloned.1.call-done = f32[320,1152]{1,0:T(8,128)} async-done(((f32[320,1152]{1,0:T(8,128)}), f32[320,1152]{1,0:T(8,128)}) %all-reduce.13.cloned.1.call-update) | async-done | bytes 1474576 | tf_op jit(solution)/shard_map/psum | solution.py:73
  863.0 4.2 fusion.20
  867.2 40.8 %all-reduce.15.cloned.1.call-done = f32[320,288]{0,1:T(8,128)} async-done(((f32[320,288]{0,1:T(8,128)}), f32[320,288]{0,1:T(8,128)}) %all-reduce.15.cloned.1.call-update) | async-done | bytes 368656 | tf_op jit(solution)/shard_map/psum | solution.py:61
  908.1 5.1 fusion.10
  913.2 2.6 fusion.15
  919.6 78.3 %all-reduce = (f32[]{:T(128)}, f32[]{:T(128)}) all-reduce(f32[]{:T(128)S(6)} %add.169, f32[]{:T(128)S(6)} %add.167), channel_id=1, replica_groups=mesh['dcn'=4,'fsdp'=16,'tp'=4] {'dcn','fsdp','tp'}, use_global_device_ids=true, to_apply=%region_31.0 | all-reduce | flops 2 | bytes 16 | tf_op jit(solution)/shard_map/psum | solution.py:65
  999.2 3.2 multiply_reduce_fusion.5
  1006.8 73.5 %psum.143 = f32[]{:T(128)} all-reduce(f32[]{:T(128)S(6)} %add.171), channel_id=1, replica_groups=mesh['dcn'=4,'fsdp'=16,'tp'=4] {'dcn','fsdp','tp'}, use_global_device_ids=true, to_apply=%region_35.0 | all-reduce | flops 1 | bytes 8 | tf_op jit(solution)/shard_map/psum | solution.py:69
  1081.0 5.4 divide_bitcast_fusion.1
  (134 shorter events, 66.2 us)
Async XLA Ops:
  7.2 99.0 %copy-start = (bf16[320,1152]{1,0:T(8,128)(2,1)S(1)}, bf16[320,1152]{1,0:T(8,128)(2,1)}, u32[]{:S(2)}) copy-start(bf16[320,1152]{1,0:T(8,128)(2,1)} %param.8) | copy-start | bytes 2211844
  10.7 9.3 copy-start.33
  10.7 32.8 %all-to-all-start.1 = ((bf16[72,16,288]{2,0,1:T(8,128)(2,1)}), bf16[72,16,288]{2,0,1:T(8,128)(2,1)S(1)}, u32[]{:S(2)}, u32[]{:S(2)}) async-start(bf16[72,16,288]{2,0,1:T(8,128)(2,1)} %copy.17), calls=%async_computation.1 | async-start | bytes 1769472 | tf_op jit(solution)/shard_map/all_to_all | solution.py:83
  43.5 27.7 %all-to-all-start.2 = ((bf16[72,16,288]{2,0,1:T(8,128)(2,1)}), bf16[72,16,288]{2,0,1:T(8,128)(2,1)S(1)}, u32[]{:S(2)}, u32[]{:S(2)}) async-start(bf16[72,16,288]{2,0,1:T(8,128)(2,1)} %copy.18), calls=%async_computation.2 | async-start | bytes 1769472 | tf_op jit(solution)/shard_map/all_to_all | solution.py:82
  71.2 6.7 copy-start.25
  71.2 27.7 %all-to-all-start = ((bf16[72,16,288]{2,0,1:T(8,128)(2,1)}), bf16[72,16,288]{2,0,1:T(8,128)(2,1)}, u32[]{:S(2)}, u32[]{:S(2)}) async-start(bf16[72,16,288]{2,0,1:T(8,128)(2,1)} %copy.16), calls=%async_computation | async-start | bytes 1769472 | tf_op jit(solution)/shard_map/all_to_all | solution.py:81
  98.9 27.1 %all-to-all-start.3 = ((bf16[72,16,288]{2,0,1:T(8,128)(2,1)}), bf16[72,16,288]{2,0,1:T(8,128)(2,1)S(1)}, u32[]{:S(2)}, u32[]{:S(2)}) async-start(bf16[72,16,288]{2,0,1:T(8,128)(2,1)} %copy.19), calls=%async_computation.3 | async-start | bytes 1769472 | tf_op jit(solution)/shard_map/all_to_all | solution.py:84
  126.1 5.8 copy-start.17
  126.1 27.3 %all-to-all-start.4 = ((bf16[16,288,72]{1,2,0:T(8,128)(2,1)}), bf16[16,288,72]{1,2,0:T(8,128)(2,1)S(1)}, u32[]{:S(2)}, u32[]{:S(2)}) async-start(bf16[16,288,72]{1,2,0:T(8,128)(2,1)} %copy.20), calls=%async_computation.4 | async-start | bytes 1769472 | tf_op jit(solution)/shard_map/all_to_all | solution.py:87
  130.0 63.7 %all-reduce.23.cloned.1.call-start = ((), (), s32[]{:S(2)}) async-start(), calls=%async_computation.11 | async-start | bytes 3538944 | tf_op jit(solution)/shard_map/psum | solution.py:57
  153.4 45.6 %all-to-all-start.5 = ((bf16[16,288,72]{1,2,0:T(8,128)(2,1)}), bf16[16,288,72]{1,2,0:T(8,128)(2,1)S(1)}, u32[]{:S(2)}, u32[]{:S(2)}) async-start(bf16[16,288,72]{1,2,0:T(8,128)(2,1)} %copy.21), calls=%async_computation.5 | async-start | bytes 1769472 | tf_op jit(solution)/shard_map/all_to_all | solution.py:88
  157.7 235.1 %all-reduce.17.cloned.1.call-start = ((), (), s32[]{:S(2)}) async-start(), calls=%async_computation.8 | async-start | bytes 5898240 | tf_op jit(solution)/shard_map/psum | solution.py:73
  202.3 245.0 %all-reduce.21.cloned.1.call-start = ((), (), s32[]{:S(2)}) async-start(), calls=%async_computation.10 | async-start | bytes 1769472 | tf_op jit(solution)/shard_map/psum | solution.py:61
  394.6 5.6 copy-start.5
  398.4 267.0 %all-reduce.19.cloned.1.call-start = ((), (), s32[]{:S(2)}) async-start(), calls=%async_computation.9 | async-start | bytes 1769472 | tf_op jit(solution)/shard_map/psum | solution.py:57
  401.8 45.5 %copy-start.24 = (f32[320,288]{0,1:T(8,128)S(1)}, f32[320,288]{0,1:T(8,128)}, u32[]{:S(2)}) copy-start(f32[320,288]{0,1:T(8,128)} %get-tuple-element.23) | copy-start | bytes 1105924
  447.3 4.5 copy-start.12
  447.3 4.5 copy-start.32
  447.3 4.5 copy-start.34
  447.3 4.5 copy-start.36
  616.0 3.0 copy-start.2
  620.4 239.2 %all-reduce.13.cloned.1.call-start = ((), (), s32[]{:S(2)}) async-start(), calls=%async_computation.6 | async-start | bytes 2949120 | tf_op jit(solution)/shard_map/psum | solution.py:73
  670.7 237.4 %all-reduce.15.cloned.1.call-start = ((), (), s32[]{:S(2)}) async-start(), calls=%async_computation.7 | async-start | bytes 884736 | tf_op jit(solution)/shard_map/psum | solution.py:61
  908.0 5.1 copy-start.3
  908.0 5.1 copy-start.15
  908.0 5.1 copy-start.35
  908.0 5.1 copy-start.37
  908.1 5.1 copy-start.38
  999.2 3.2 copy-start.4
  999.2 3.2 copy-start.16
  999.2 3.2 copy-start.23
  1081.0 5.4 copy-start.22
  (19 other events, 31.6 us)
Sparse Core Ops, SparseCore 0:
  133.4 60.2 all-reduce.22
  202.5 190.3 all-reduce.16
  398.5 48.7 all-reduce.20
  620.5 44.8 all-reduce.18
  670.8 188.7 all-reduce.12
  863.1 44.8 all-reduce.14
where the time goes:
time: 1110 us; the launch traced here: 1100 us
  waiting for transfers between devices  627 us (56%)
  blocking collectives  303 us (27%)
  matrix products  52.4 us (5%)
  between operations  31.4 us (3%)
  starting transfers between devices  30.4 us (3%)
  local copies, waits for them, and re-layouts  26.4 us (2%)
  other arithmetic  25.9 us (2%)
    psum x2, waiting for transfers between devices, out_grad(): whole = lax.psum(partial_out, ('fsdp', 'tp'))  368 us
    psum x2, blocking collectives, projections(): return lax.psum((values[0], values[1]), ('dcn', 'fsdp', 'tp'))  156 us
    psum x2, blocking collectives, residual_norm(): return lax.psum(value, ('dcn', 'fsdp', 'tp'))  147 us
    psum x2, waiting for transfers between devices, back_sum(): return lax.psum(partial_grad, 'dcn')  84.1 us
    psum x2, waiting for transfers between devices, feature_sum(): return lax.psum((former, latter), 'dcn')  80.9 us
    dot_general x8, matrix products, contract_first(): lax.dot_general(former, latter, (((0,), (0,)), ((), ())), preferred_eleme...  25.4 us
  transfers between devices with their start and end apart: 12, of which 11 were waited for; matrix products, arithmetic and copies ran while one was open for 3% of the time, Pallas kernels for 0%

commit v1 on v0

v1 whole, which is shorter than its diff:
```python
import math

import jax
import jax.numpy as jnp
from jax import lax
from jax.experimental import pallas as pl
from jax.experimental.pallas import tpu as pltpu
from jax.sharding import PartitionSpec as P

D = 4608
FF = 18432
TOK = 320
DB = 1152
HB = 288
TQ = 80
RQ = 16
NRED = 5
LO = 640
LS = 512
BLK = 144
ENTRIES = float(3 * D * FF)
EPS = 1e-06
SCALE = 2.0**-14
MESH = pl.DeviceIdType.MESH
BF = jnp.bfloat16
F32 = jnp.float32

gelu_cubic = 0.044715
gelu_scale = math.sqrt(2.0 / math.pi)


def gelu_parts(argument):
    squared = argument * argument
    inner_arg = gelu_scale * (argument + gelu_cubic * squared * argument)
    tanh_val = jnp.tanh(inner_arg)
    sech_square = 1.0 - tanh_val * tanh_val
    inner_slope = gelu_scale * (1.0 + 3.0 * gelu_cubic * squared)
    inner_curve = gelu_scale * 6.0 * gelu_cubic * argument
    gelu_val = 0.5 * argument * (1.0 + tanh_val)
    gelu_slope = 0.5 * (1.0 + tanh_val) + 0.5 * argument * sech_square * inner_slope
    gelu_curve = sech_square * inner_slope + 0.5 * argument * (
        sech_square * inner_curve - 2.0 * tanh_val * sech_square * inner_slope * inner_slope
    )
    return (gelu_val, gelu_slope, gelu_curve)


def nn(a, b):
    return lax.dot_general(a, b, (((1,), (0,)), ((), ())), preferred_element_type=F32)


def nt(a, b):
    return lax.dot_general(a, b, (((1,), (1,)), ((), ())), preferred_element_type=F32)


def tn(a, b):
    return lax.dot_general(a, b, (((0,), (0,)), ((), ())), preferred_element_type=F32)


class Place:
    def __init__(self):
        self.x = lax.axis_index("dcn")
        fsdp = lax.axis_index("fsdp")
        tp = lax.axis_index("tp")
        self.y = fsdp // 4
        self.z = (tp // 2) * 4 + fsdp % 4
        self.c = tp % 2

    def dev(self, x=None, y=None, z=None, c=None):
        x = self.x if x is None else x
        y = self.y if y is None else y
        z = self.z if z is None else z
        c = self.c if c is None else c
        return (x, y * 4 + z % 4, (z // 4) * 2 + c)

    def at_x(self, k):
        return self.dev(x=(self.x + k) % 4)

    def at_y(self, k):
        return self.dev(y=(self.y + k) % 4)

    def at_z(self, k):
        return self.dev(z=(self.z + k) % 8)

    def other(self):
        return self.dev(c=1 - self.c)


def rows_of(index, size):
    return pl.ds(pl.multiple_of(index * size, size), size)


def lanes_of(index, step, size):
    return pl.ds(pl.multiple_of(index * step, 128), size)


def remote(src, dst, ssem, rsem, dev):
    return pltpu.make_async_remote_copy(
        src_ref=src, dst_ref=dst, send_sem=ssem, recv_sem=rsem, device_id=dev, device_id_type=MESH
    )


class Flight:
    def __init__(self):
        self.sent = []

    def start(self, src, dst, ssem, rsem, dev):
        copy = remote(src, dst, ssem, rsem, dev)
        copy.start()
        self.sent.append(copy)
        return copy


def scatter_x(me, fl, stage, slots, sems):
    out = []
    for k in (1, 2, 3):
        peer = (me.x + k) % 4
        out.append(
            fl.start(
                stage.at[:, rows_of(peer, TQ), :],
                slots.at[k - 1],
                sems.at[0, k - 1],
                sems.at[1, k - 1],
                me.at_x(k),
            )
        )
    return out


def gather_x(me, fl, buf, sems):
    out = []
    mine = buf.at[:, rows_of(me.x, TQ), :]
    for k in (1, 2, 3):
        out.append(fl.start(mine, mine, sems.at[0, k - 1], sems.at[1, k - 1], me.at_x(k)))
    return out


def landed(copies):
    for copy in copies:
        copy.wait_recv()


class Reduce64:
    def __init__(self, me, fl, n, s):
        self.me, self.fl, self.n = me, fl, n
        (self.acc, self.send, self.r1, self.t1, self.t1b, self.r2, self.t2, self.t2b, self.r3, self.sems) = s

    def put(self, index, value):
        self.acc[index] = value
        self.send[index] = value.astype(BF)

    def cores(self):
        me = self.me
        self.c1 = self.fl.start(
            self.send.at[:, :, lanes_of(1 - me.c, LS, LO)],
            self.r1,
            self.sems.at[0, 0],
            self.sems.at[1, 0],
            me.other(),
        )

    def ys(self):
        me = self.me
        self.c1.wait_recv()
        for i in range(self.n):
            total = self.acc[i, :, lanes_of(me.c, LS, LO)] + self.r1[i].astype(F32)
            self.t1[i] = total
            self.t1b[i] = total.astype(BF)
        self.c2 = []
        for k in (1, 2, 3):
            peer = (me.y + k) % 4
            self.c2.append(
                self.fl.start(
                    self.t1b.at[:, rows_of(peer, TQ), :],
                    self.r2.at[k - 1],
                    self.sems.at[0, k],
                    self.sems.at[1, k],
                    me.at_y(k),
                )
            )

    def zs(self):
        me = self.me
        landed(self.c2)
        for i in range(self.n):
            total = self.t1[i, rows_of(me.y, TQ), :]
            for k in range(3):
                total = total + self.r2[k, i].astype(F32)
            self.t2b[i] = total.astype(BF)
        for q in range(NRED):

            @pl.when(me.z != q)
            def _():
                remote(
                    self.t2b.at[:, q * RQ : (q + 1) * RQ, :],
                    self.r3.at[me.z],
                    self.sems.at[0, 4 + q],
                    self.sems.at[1, 4 + me.z],
                    me.dev(z=q),
                ).start()

    def finish(self, final, post):
        me = self.me
        mine = lanes_of(me.c, LS, LO)

        @pl.when(me.z < NRED)
        def _():
            self.r3[me.z] = self.t2b[:, rows_of(me.z, RQ), :]
            for s in range(8):

                @pl.when(me.z != s)
                def _():
                    remote(
                        self.t2b.at[:, 0:RQ, :],
                        self.r3.at[s],
                        self.sems.at[0, 4],
                        self.sems.at[1, 4 + s],
                        me.other(),
                    ).wait_recv()

            rows = pl.ds(pl.multiple_of(me.y * TQ + me.z * RQ, RQ), RQ)
            for i in range(self.n):
                total = self.r3[0, i].astype(F32)
                for s in range(1, 8):
                    total = total + self.r3[s, i].astype(F32)
                final[i, rows, mine] = post(i, total, rows, mine)
            for k in range(1, 8):
                piece = final.at[:, rows, mine]
                remote(piece, piece, self.sems.at[0, 11 + k], self.sems.at[1, 12 + me.z], me.at_z(k)).start()

        for q in range(NRED):
            piece = final.at[:, pl.ds(pl.multiple_of(me.y * TQ + q * RQ, RQ), RQ), mine]

            @pl.when(me.z != q)
            def _():
                remote(piece, piece, self.sems.at[0, 4], self.sems.at[1, 12 + q], me.other()).wait_recv()

        block = final.at[:, rows_of(me.y, TQ), mine]
        c5 = []
        for k in (1, 2, 3):
            c5.append(
                self.fl.start(block, block, self.sems.at[0, 19 + k], self.sems.at[1, 19 + k], me.at_y(k))
            )
        landed(c5)
        half = final.at[:, :, lanes_of(me.c, LO, LS)]
        c6 = self.fl.start(half, half, self.sems.at[0, 23], self.sems.at[1, 23], me.other())
        c6.wait_recv()

    def drain(self):
        me = self.me
        for q in range(NRED):

            @pl.when(me.z != q)
            def _():
                remote(
                    self.t2b.at[:, q * RQ : (q + 1) * RQ, :],
                    self.r3.at[me.z],
                    self.sems.at[0, 4 + q],
                    self.sems.at[1, 4 + me.z],
                    me.dev(z=q),
                ).wait_send()

        @pl.when(me.z < NRED)
        def _():
            for k in range(1, 8):
                remote(
                    self.t2b.at[:, 0:RQ, :],
                    self.t2b.at[:, 0:RQ, :],
                    self.sems.at[0, 11 + k],
                    self.sems.at[1, 12],
                    me.other(),
                ).wait_send()


def reduce_scratch(n):
    return [
        pltpu.VMEM((n, TOK, DB), F32),
        pltpu.VMEM((n, TOK, DB), BF),
        pltpu.VMEM((n, TOK, LO), BF),
        pltpu.VMEM((n, TOK, LO), F32),
        pltpu.VMEM((n, TOK, LO), BF),
        pltpu.VMEM((3, n, TQ, LO), BF),
        pltpu.VMEM((n, TQ, LO), F32),
        pltpu.VMEM((n, TQ, LO), BF),
        pltpu.VMEM((8, n, RQ, LO), BF),
        pltpu.SemaphoreType.DMA((2, 24)),
    ]


class ScalarSum:
    def __init__(self, me, fl, buf, sems):
        self.me, self.fl, self.buf, self.sems = me, fl, buf, sems

    def go(self, stage, tile):
        me = self.me
        count, index, base, at = (
            (2, me.c, 0, lambda k: me.other()),
            (4, me.x, 2, me.at_x),
            (4, me.y, 6, me.at_y),
            (8, me.z, 10, me.at_z),
        )[stage]
        mine = self.buf.at[base + index]
        self.buf[base + index] = tile
        self.copies = []
        for k in range(1, count):
            self.copies.append(
                self.fl.start(mine, mine, self.sems.at[0, base + k], self.sems.at[1, base + k], at(k))
            )
        self.span = (base, count)

    def get(self):
        landed(self.copies)
        base, count = self.span
        total = self.buf[base]
        for s in range(1, count):
            total = total + self.buf[base + s]
        return total


def rsqrt_of(value):
    return 1.0 / jnp.sqrt(value)


def whole_sum(value):
    return jnp.sum(jnp.sum(value, axis=1, keepdims=True), axis=0, keepdims=True)


def fold(value):
    return jnp.sum(value.reshape(BLK // 8, 8, HB), axis=0)


def tile_of(values):
    rows = [jnp.broadcast_to(v, (1, 128)) for v in values]
    while len(rows) < 8:
        rows.append(jnp.zeros((1, 128), F32))
    return jnp.concatenate(rows, axis=0)


def kernel(
    x, x_t, target, w_gate, w_up, w_down, s_gate, s_up, s_down,
    one, two, scal,
    kp, kr, kpair, sems_k,
    acc_a, send_a, slots_a, sems_a,
    own, hh, sems_h, mm, sems_m,
    red_b0, red_b1, red_b2, red_b3, red_b4, red_b5, red_b6, red_b7, red_b8, red_b9,
    gg,
    acc_c, send_c, slots_c, sems_c,
    gu1, sems_g1, u1d, tan2, h2,
    red_e0, red_e1, red_e2, red_e3, red_e4, red_e5, red_e6, red_e7, red_e8, red_e9,
    g2,
    acc_f, send_f, slots_f, sems_f,
    gu2, sems_g2,
    sbuf1, ssem1, sbuf2, ssem2,
):
    me = Place()
    fl = Flight()
    starts = (s_gate, s_up, s_down)

    barrier = pltpu.get_barrier_semaphore()
    peers = (
        [me.at_x(k) for k in (1, 2, 3)]
        + [me.at_y(k) for k in (1, 2, 3)]
        + [me.at_z(k) for k in range(1, 8)]
        + [me.other()]
    )
    for peer in peers:
        pl.semaphore_signal(barrier, inc=1, device_id=peer, device_id_type=MESH)

    for i, w in enumerate((w_gate, w_up, s_gate, s_up)):
        part = nn(x[...], w[...])
        acc_a[i] = part
        send_a[i] = part.astype(BF)
    kp[...] = nt(x[...], x[...])
    pl.semaphore_wait(barrier, len(peers))
    c_a = scatter_x(me, fl, send_a, slots_a, sems_a)
    c_k = []
    for k in (1, 2, 3):
        c_k.append(fl.start(kp, kr.at[k - 1], sems_k.at[0, k - 1], sems_k.at[1, k - 1], me.at_x(k)))

    landed(c_a)
    my_rows = rows_of(me.x, TQ)
    sums = []
    for i in range(4):
        total = acc_a[i, my_rows, :]
        for k in range(3):
            total = total + slots_a[k, i].astype(F32)
        sums.append(total)
    gate_pre, up_pre, gate_dot, up_dot = sums
    val, slope, curve = gelu_parts(gate_pre)
    slope_up = slope * up_pre
    hh[0, my_rows, :] = (val * up_pre).astype(BF)
    hh[1, my_rows, :] = (slope_up * gate_dot + val * up_dot).astype(BF)
    c_h = gather_x(me, fl, hh, sems_h)
    mm[0, my_rows, :] = slope_up
    mm[1, my_rows, :] = val
    c_m = gather_x(me, fl, mm, sems_m)
    own[0] = slope
    own[1] = up_pre * curve
    own[2] = gate_dot
    own[3] = up_dot
    landed(c_h)

    red = Reduce64(
        me, fl, 2, (red_b0, red_b1, red_b2, red_b3, red_b4, red_b5, red_b6, red_b7, red_b8, red_b9)
    )
    red.put(0, nt(hh[0], w_down[...]))
    red.put(1, nt(hh[1], w_down[...]) + nt(hh[0], s_down[...]))
    red.cores()
    red.ys()
    landed(c_k)
    total = kp[...] + (kr[0] + kr[1] + kr[2])
    high = total.astype(BF)
    kpair[0] = high
    kpair[1] = (total - high.astype(F32)).astype(BF)
    red.zs()

    def first_post(i, total, rows, lanes):
        if i == 0:
            total = total - target[rows, lanes].astype(F32)
        return (total / float(TOK)).astype(BF)

    red.finish(gg, first_post)

    part = nn(gg[0], w_down[...])
    acc_c[0] = part
    send_c[0] = part.astype(BF)
    part = nn(gg[1], w_down[...]) + nn(gg[0], s_down[...])
    acc_c[1] = part
    send_c[1] = part.astype(BF)
    c_c = scatter_x(me, fl, send_c, slots_c, sems_c)
    part = tn(gg[0], hh[1]) + tn(gg[1], hh[0])
    one[2] = part
    u1d[...] = part.astype(BF)
    landed(c_c)
    sums = []
    for i in range(2):
        total = acc_c[i, my_rows, :]
        for k in range(3):
            total = total + slots_c[k, i].astype(F32)
        sums.append(total)
    grad_hidden, back_dot = sums
    slope_term = grad_hidden * own[0]
    curve_term = grad_hidden * own[1]
    own[0] = slope_term
    own[1] = curve_term
    gu1[0, my_rows, :] = (
        back_dot * mm[0, my_rows, :] + slope_term * own[3] + curve_term * own[2]
    ).astype(BF)
    gu1[1, my_rows, :] = (back_dot * mm[1, my_rows, :] + slope_term * own[2]).astype(BF)
    c_g1 = gather_x(me, fl, gu1, sems_g1)
    landed(c_m)
    landed(c_g1)

    for i in range(2):
        tan2[i] = nn(kpair[0], gu1[i]) + nn(kpair[1], gu1[i])
    h2[...] = (mm[0] * tan2[0] + mm[1] * tan2[1]).astype(BF)
    red2 = Reduce64(
        me, fl, 1, (red_e0, red_e1, red_e2, red_e3, red_e4, red_e5, red_e6, red_e7, red_e8, red_e9)
    )
    red2.put(0, nt(h2[...], w_down[...]) + nt(hh[0], u1d[...]))
    red2.cores()
    red2.ys()
    for i in range(2):
        one[i] = nn(x_t[...], gu1[i])

    def dots_one(b, carry):
        rows = rows_of(b, BLK)
        ss, su, uu = carry
        for i in range(3):
            s = starts[i][rows, :].astype(F32) * SCALE
            u = one[i, rows, :] * SCALE
            ss = ss + fold(s * s)
            su = su + fold(s * u)
            uu = uu + fold(u * u)
        return ss, su, uu

    zero = jnp.zeros((8, HB), F32)
    ss, su, uu = lax.fori_loop(0, DB // BLK, dots_one, (zero, zero, zero))
    red2.zs()
    sum1 = ScalarSum(me, fl, sbuf1, ssem1)
    sum1.go(0, tile_of([whole_sum(ss), whole_sum(su), whole_sum(uu)]))
    sum1.go(1, sum1.get())
    red2.finish(g2, lambda i, total, rows, lanes: (total / float(TOK)).astype(BF))

    part = nn(g2[0], w_down[...]) + nn(gg[0], u1d[...])
    acc_f[0] = part
    send_f[0] = part.astype(BF)
    c_f = scatter_x(me, fl, send_f, slots_f, sems_f)
    sum1.go(2, sum1.get())
    two[2] = tn(gg[0], h2[...]) + tn(g2[0], hh[0])
    landed(c_f)
    back_dot = acc_f[0, my_rows, :]
    for k in range(3):
        back_dot = back_dot + slots_f[k, 0].astype(F32)
    gate_two = tan2[0, my_rows, :]
    up_two = tan2[1, my_rows, :]
    gu2[0, my_rows, :] = (
        back_dot * mm[0, my_rows, :] + own[0] * up_two + own[1] * gate_two
    ).astype(BF)
    gu2[1, my_rows, :] = (back_dot * mm[1, my_rows, :] + own[0] * gate_two).astype(BF)
    c_g2 = gather_x(me, fl, gu2, sems_g2)
    sum1.go(3, sum1.get())
    norms = sum1.get() * (1.0 / (SCALE * SCALE * ENTRIES))
    s_s, s_u, u_u = norms[0:1, 0:1], norms[1:2, 0:1], norms[2:3, 0:1]
    f = 1.0 / jnp.sqrt(s_s + EPS)
    v11 = f * f * s_s
    h11 = f * f * s_u
    w11 = f * f * u_u
    rr = jnp.maximum(w11 - h11 * h11 * (2.0 - v11), 0.0)
    h21 = jnp.sqrt(rr + EPS)
    v12 = (h11 - h11 * v11) / h21
    v22 = rr / (h21 * h21)
    a1 = f / h21
    a0 = -h11 * f / h21
    landed(c_g2)
    for i in range(2):
        two[i] = nn(x_t[...], gu2[i])

    def dots_two(b, carry):
        rows = rows_of(b, BLK)
        p1, p2, pw = carry
        for i in range(3):
            s = starts[i][rows, :].astype(F32)
            u = one[i, rows, :]
            w = (a1 * two[i, rows, :] + a0 * u) * SCALE
            first = f * s * SCALE
            second = (a1 * u + a0 * s) * SCALE
            p1 = p1 + fold(first * w)
            p2 = p2 + fold(second * w)
            pw = pw + fold(w * w)
        return p1, p2, pw

    p1, p2, pw = lax.fori_loop(0, DB // BLK, dots_two, (zero, zero, zero))
    sum2 = ScalarSum(me, fl, sbuf2, ssem2)
    tile = tile_of([whole_sum(p1), whole_sum(p2), whole_sum(pw)])
    for stage in range(4):
        sum2.go(stage, tile)
        tile = sum2.get()
    norms = tile * (1.0 / (SCALE * SCALE * ENTRIES))
    h12, h22, ww = norms[0:1, 0:1], norms[1:2, 0:1], norms[2:3, 0:1]
    rr = (
        ww
        - 2.0 * (h12 * h12 + h22 * h22)
        + h12 * h12 * v11
        + h22 * h22 * v22
        + 2.0 * h12 * h22 * v12
    )
    h32 = jnp.sqrt(jnp.maximum(rr, 0.0) + EPS)
    c2 = a1 / h32
    c1 = (a0 - h22 * a1) / h32
    c0 = -(h12 * f + h22 * a0) / h32
    scal[...] = tile_of([h21, h12, h22, h32, h11, c2, c1, c0])

    for copy in fl.sent:
        copy.wait_send()
    red.drain()
    red2.drain()


def rounds(*operands):
    dma = pltpu.SemaphoreType.DMA
    scratch = (
        [pltpu.VMEM((TOK, TOK), F32), pltpu.VMEM((3, TOK, TOK), F32), pltpu.VMEM((2, TOK, TOK), BF), dma((2, 3))]
        + [pltpu.VMEM((4, TOK, HB), F32), pltpu.VMEM((4, TOK, HB), BF), pltpu.VMEM((3, 4, TQ, HB), BF), dma((2, 3))]
        + [pltpu.VMEM((4, TQ, HB), F32), pltpu.VMEM((2, TOK, HB), BF), dma((2, 3)), pltpu.VMEM((2, TOK, HB), F32), dma((2, 3))]
        + reduce_scratch(2)
        + [pltpu.VMEM((2, TOK, DB), BF)]
        + [pltpu.VMEM((2, TOK, HB), F32), pltpu.VMEM((2, TOK, HB), BF), pltpu.VMEM((3, 2, TQ, HB), BF), dma((2, 3))]
        + [pltpu.VMEM((2, TOK, HB), BF), dma((2, 3)), pltpu.VMEM((DB, HB), BF), pltpu.VMEM((2, TOK, HB), F32), pltpu.VMEM((TOK, HB), BF)]
        + reduce_scratch(1)
        + [pltpu.VMEM((1, TOK, DB), BF)]
        + [pltpu.VMEM((1, TOK, HB), F32), pltpu.VMEM((1, TOK, HB), BF), pltpu.VMEM((3, 1, TQ, HB), BF), dma((2, 3))]
        + [pltpu.VMEM((2, TOK, HB), BF), dma((2, 3))]
        + [pltpu.VMEM((18, 8, 128), F32), dma((2, 18)), pltpu.VMEM((18, 8, 128), F32), dma((2, 18))]
    )
    return pl.pallas_call(
        kernel,
        out_shape=(
            jax.ShapeDtypeStruct((3, DB, HB), F32),
            jax.ShapeDtypeStruct((3, DB, HB), F32),
            jax.ShapeDtypeStruct((8, 128), F32),
        ),
        in_specs=[pl.BlockSpec(memory_space=pltpu.VMEM)] * 9,
        out_specs=[pl.BlockSpec(memory_space=pltpu.VMEM)] * 3,
        scratch_shapes=scratch,
        compiler_params=pltpu.CompilerParams(
            collective_id=0, has_side_effects=True, vmem_limit_bytes=58 * 1024 * 1024
        ),
        name="arnoldi",
    )(*operands)


def on_device(inputs, target, w_gate, w_up, w_down, start_gate, start_up, start_down):
    def regroup(w):
        return lax.all_to_all(w, "fsdp", split_axis=1, concat_axis=0, tiled=True)

    gate_cols, up_cols, start_gcols, start_ucols = map(regroup, (w_gate, w_up, start_gate, start_up))
    down_cols, start_dcols = map(regroup, (w_down.T, start_down.T))
    one, two, scal = rounds(
        inputs, inputs.T, target, gate_cols, up_cols, down_cols, start_gcols, start_ucols, start_dcols
    )
    c2, c1, c0 = scal[5, 0], scal[6, 0], scal[7, 0]
    third = [
        c2 * two[i] + c1 * one[i] + c0 * s.astype(F32)
        for i, s in enumerate((start_gcols, start_ucols, start_dcols))
    ]
    return (
        third[0].reshape(DB, 1, HB),
        third[1].reshape(DB, 1, HB),
        third[2].T.reshape(1, HB, DB),
        scal[0:4, 0],
        scal[4:5, 0],
    )


def solution(mesh):
    placed = (
        P(None, "dcn"),
        P(None, "dcn"),
        P(("dcn", "fsdp"), "tp"),
        P(("dcn", "fsdp"), "tp"),
        P("tp", ("dcn", "fsdp")),
        P(("dcn", "fsdp"), "tp"),
        P(("dcn", "fsdp"), "tp"),
        P("tp", ("dcn", "fsdp")),
    )
    return jax.shard_map(
        on_device,
        mesh=mesh,
        in_specs=placed,
        out_specs=(
            P("dcn", "tp", "fsdp"),
            P("dcn", "tp", "fsdp"),
            P("tp", "fsdp", "dcn"),
            P(),
            P(),
        ),
        check_vma=False,
    )
```

time: 1110 us -> 374 us (0.34)
  waiting for transfers between devices: 627 us -> 128 us
  blocking collectives: 303 us -> 0 us
  Pallas kernels: 0 us -> 177 us
  matrix products: 52.4 us -> 0 us
  between operations: 31.4 us -> 0.86 us
  other arithmetic: 25.9 us -> 9.64 us
    psum x6 -> x0, waiting for transfers between devices: 533 us -> none  [the longest x2 368 us: out_grad(): whole = lax.psum(partial_out, ('fsdp', 'tp'))]
    psum x4 -> x0, blocking collectives: 303 us -> none  [the longest x2 156 us: projections(): return lax.psum((values[0], values[1]), ('dcn', 'fsdp', 'tp'))]
    pallas_call x0 -> x1, Pallas kernels: none -> 177 us  [rounds(): pl.pallas_call(kernel, out_shape=(jax.ShapeDtypeStruct((3, DB, HB), F32),...]
    dot_general x24 -> x0, matrix products: 52.4 us -> none  [the longest x8 25.4 us: contract_first(): lax.dot_general(former, latter, (((0,), (0,)), ((), ())), preferred_eleme...]
    all_to_all x6, waiting for transfers between devices: 93.8 us -> 128 us  [regroup(): return lax.all_to_all(w, 'fsdp', split_axis=1, concat_axis=0, tiled=True)]
    reduce_sum x9 -> x0, other arithmetic: 13.2 us -> none  [the longest x3 6.86 us: local_dot(): jnp.sum(former[0] * latter[0]) + jnp.sum(former[1] * latter[1])]
    all_to_all x15 -> x12, local copies, waits for them, and re-layouts: 24.2 us -> 15 us  [regroup(): return lax.all_to_all(w, 'fsdp', split_axis=1, concat_axis=0, tiled=True)]
  transfers between devices with their start and end apart: 12 -> 6, of which waited for: 11 -> 6; matrix products, arithmetic and copies ran while one was open for 3% -> 2% of each run, Pallas kernels for 0% -> 0%
where the time goes in v1:
time: 374 us; the launch traced here: 372 us
  Pallas kernels  177 us (47%)
  waiting for transfers between devices  128 us (34%)
  starting transfers between devices  30.1 us (8%)
  local copies, waits for them, and re-layouts  26.2 us (7%)
  other arithmetic  9.64 us (3%)
    pallas_call x1, Pallas kernels, rounds(): pl.pallas_call(kernel, out_shape=(jax.ShapeDtypeStruct((3, DB, HB), F32),...  177 us
    all_to_all x6, waiting for transfers between devices, regroup(): return lax.all_to_all(w, 'fsdp', split_axis=1, concat_axis=0, tiled=True)  128 us
    all_to_all x6, starting transfers between devices, regroup(): return lax.all_to_all(w, 'fsdp', split_axis=1, concat_axis=0, tiled=True)  30.1 us
    all_to_all x12, local copies, waits for them, and re-layouts, regroup(): return lax.all_to_all(w, 'fsdp', split_axis=1, concat_axis=0, tiled=True)  15 us
    unnamed x36, local copies, waits for them, and re-layouts  8.45 us
  transfers between devices with their start and end apart: 6, of which 6 were waited for; matrix products, arithmetic and copies ran while one was open for 2% of the time, Pallas kernels for 0%

profile of v1, /device:TPU:1, one launch (start us, length us, event | category | flops | bytes accessed | tf_op | source)
XLA Modules:
  0.0 371.8 jit_solution(13442679792748864380)
XLA Ops:
  0.6 2.4 all_to_all.100
  3.0 1.1 copy.28
  4.1 9.2 %all-to-all-start.4 = ((bf16[72,16,288]{2,0,1:T(8,128)(2,1)}), bf16[72,16,288]{2,0,1:T(8,128)(2,1)S(1)}, u32[]{:S(2)}, u32[]{:S(2)}) async-start(bf16[72,16,288]{2,0,1:T(8,128)(2,1)} %copy.28), calls=%async_computation.4 | async-start | bytes 1769472 | tf_op jit(solution)/shard_map/all_to_all | solution.py:594
  13.3 1.2 all_to_all.104
  14.5 1.1 copy.29
  15.6 21.1 %all-to-all-done.4 = bf16[72,16,288]{2,0,1:T(8,128)(2,1)S(1)} async-done(((bf16[72,16,288]{2,0,1:T(8,128)(2,1)}), bf16[72,16,288]{2,0,1:T(8,128)(2,1)S(1)}, u32[]{:S(2)}, u32[]{:S(2)}) %all-to-all-start.4) | async-done | bytes 663584 | tf_op jit(solution)/shard_map/all_to_all | solution.py:594
  36.8 4.2 %all-to-all-start.5 = ((bf16[72,16,288]{2,0,1:T(8,128)(2,1)}), bf16[72,16,288]{2,0,1:T(8,128)(2,1)S(1)}, u32[]{:S(2)}, u32[]{:S(2)}) async-start(bf16[72,16,288]{2,0,1:T(8,128)(2,1)} %copy.29), calls=%async_computation.5 | async-start | bytes 1769472 | tf_op jit(solution)/shard_map/all_to_all | solution.py:594
  41.0 1.2 all_to_all.96
  43.3 21.1 %all-to-all-done.5 = bf16[72,16,288]{2,0,1:T(8,128)(2,1)S(1)} async-done(((bf16[72,16,288]{2,0,1:T(8,128)(2,1)}), bf16[72,16,288]{2,0,1:T(8,128)(2,1)S(1)}, u32[]{:S(2)}, u32[]{:S(2)}) %all-to-all-start.5) | async-done | bytes 663584 | tf_op jit(solution)/shard_map/all_to_all | solution.py:594
  64.5 4.2 %all-to-all-start.3 = ((bf16[72,16,288]{2,0,1:T(8,128)(2,1)}), bf16[72,16,288]{2,0,1:T(8,128)(2,1)S(1)}, u32[]{:S(2)}, u32[]{:S(2)}) async-start(bf16[72,16,288]{2,0,1:T(8,128)(2,1)} %copy.27), calls=%async_computation.3 | async-start | bytes 1769472 | tf_op jit(solution)/shard_map/all_to_all | solution.py:594
  68.7 1.2 all_to_all.84
  71.0 21.1 %all-to-all-done.3 = bf16[72,16,288]{2,0,1:T(8,128)(2,1)S(1)} async-done(((bf16[72,16,288]{2,0,1:T(8,128)(2,1)}), bf16[72,16,288]{2,0,1:T(8,128)(2,1)S(1)}, u32[]{:S(2)}, u32[]{:S(2)}) %all-to-all-start.3) | async-done | bytes 663584 | tf_op jit(solution)/shard_map/all_to_all | solution.py:594
  92.1 4.2 %all-to-all-start = ((bf16[72,16,288]{2,0,1:T(8,128)(2,1)}), bf16[72,16,288]{2,0,1:T(8,128)(2,1)S(1)}, u32[]{:S(2)}, u32[]{:S(2)}) async-start(bf16[72,16,288]{2,0,1:T(8,128)(2,1)} %copy.24), calls=%async_computation | async-start | bytes 1769472 | tf_op jit(solution)/shard_map/all_to_all | solution.py:594
  96.3 1.2 all_to_all.88
  97.6 1.1 copy.25
  98.7 21.1 %all-to-all-done = bf16[72,16,288]{2,0,1:T(8,128)(2,1)S(1)} async-done(((bf16[72,16,288]{2,0,1:T(8,128)(2,1)}), bf16[72,16,288]{2,0,1:T(8,128)(2,1)S(1)}, u32[]{:S(2)}, u32[]{:S(2)}) %all-to-all-start) | async-done | bytes 663584 | tf_op jit(solution)/shard_map/all_to_all | solution.py:594
  119.8 4.2 %all-to-all-start.1 = ((bf16[72,16,288]{2,0,1:T(8,128)(2,1)}), bf16[72,16,288]{2,0,1:T(8,128)(2,1)S(1)}, u32[]{:S(2)}, u32[]{:S(2)}) async-start(bf16[72,16,288]{2,0,1:T(8,128)(2,1)} %copy.25), calls=%async_computation.1 | async-start | bytes 1769472 | tf_op jit(solution)/shard_map/all_to_all | solution.py:594
  124.0 1.2 all_to_all.92
  125.2 1.1 copy.26
  126.4 21.1 %all-to-all-done.1 = bf16[72,16,288]{2,0,1:T(8,128)(2,1)S(1)} async-done(((bf16[72,16,288]{2,0,1:T(8,128)(2,1)}), bf16[72,16,288]{2,0,1:T(8,128)(2,1)S(1)}, u32[]{:S(2)}, u32[]{:S(2)}) %all-to-all-start.1) | async-done | bytes 663584 | tf_op jit(solution)/shard_map/all_to_all | solution.py:594
  147.5 4.2 %all-to-all-start.2 = ((bf16[72,16,288]{2,0,1:T(8,128)(2,1)}), bf16[72,16,288]{2,0,1:T(8,128)(2,1)S(1)}, u32[]{:S(2)}, u32[]{:S(2)}) async-start(bf16[72,16,288]{2,0,1:T(8,128)(2,1)} %copy.26), calls=%async_computation.2 | async-start | bytes 1769472 | tf_op jit(solution)/shard_map/all_to_all | solution.py:594
  151.7 1.3 copy.23
  153.0 22.1 %all-to-all-done.2 = bf16[72,16,288]{2,0,1:T(8,128)(2,1)S(1)} async-done(((bf16[72,16,288]{2,0,1:T(8,128)(2,1)}), bf16[72,16,288]{2,0,1:T(8,128)(2,1)S(1)}, u32[]{:S(2)}, u32[]{:S(2)}) %all-to-all-start.2) | async-done | bytes 663584 | tf_op jit(solution)/shard_map/all_to_all | solution.py:594
  176.1 177.2 %arnoldi.1 = (f32[3,1152,288]{2,1,0:T(8,128)}, f32[3,1152,288]{2,1,0:T(8,128)}, f32[8,128]{1,0:T(8,128)}) custom-call(bf16[320,1152]{1,0:T(8,128)(2,1)} %x.1, bf16[1152,320]{1,0:T(8,128)(2,1)} %bitcast.50, bf16[320,1152]{1,0:T(8,128)(2,1)} %target.1, bf16[1152,288]{1,0:T(8,128)(2,1)} %bitcast.47, bf16[1152,288]{1,0:T(8,128)(2,1)} %bitcast.48, ...), custom_call_target="tpu_custom_call" | custom-call | tf_op jit(solution)/shard_map/arnoldi/pallas_call | solution.py:575
  353.3 1.4 fusion.1
  354.7 1.3 slice_reduce_fusion
  357.1 1.4 copy-done.6
  358.5 4.2 %bitcast_add_fusion.1 = (f32[1152,1,288]{2,0,1:T(8,128)S(1)}, f32[1152,1,288]{2,0,1:T(8,128)S(1)}) fusion(f32[16,72,288]{2,1,0:T(8,128)S(1)} %get-tuple-element.27, f32[3,1152,288]{2,1,0:T(8,128)S(1)} %copy-done.6, f32[3,1152,288]{2,1,0:T(8,128)} %get-tuple-element.9, f32[]{:T(128)} %bitcast.16, f32[]{:T(128)} %bitcast.15, ...), kind=kLoop, calls=%fused_computation.2 | loop fusion | flops 2654208 | bytes 10616840 | tf_op jit(solution)/shard_map/add | solution.py:603
  362.7 1.6 copy.30
  364.3 1.6 copy.31
  365.9 4.3 %fusion = f32[1,288,1152]{1,2,0:T(8,128)S(1)} fusion(f32[3,1152,288]{2,1,0:T(8,128)} %get-tuple-element.10, f32[3,1152,288]{2,1,0:T(8,128)} %get-tuple-element.9, f32[]{:T(128)} %bitcast.18, f32[]{:T(128)} %bitcast.16, f32[]{:T(128)} %bitcast.15, bf16[72,16,288]{2,0,1:T(8,128)(2,1)S(1)} %copy-done.1), kind=kLoop, calls=%fused_computation.1 | loop fusion | flops 1990656 | bytes 4644876 | tf_op jit(solution)/shard_map/reshape | solution.py:609
  370.2 1.6 copy.32
  (34 shorter events, 4.2 us)
Async XLA Ops:
  3.0 10.3 %copy-start.11 = (bf16[4608,72]{0,1:T(8,128)(2,1)S(1)}, bf16[4608,72]{0,1:T(8,128)(2,1)}, u32[]{:S(2)}) copy-start(bf16[4608,72]{0,1:T(8,128)(2,1)} %param.15) | copy-start | bytes 1990660
  4.1 32.7 %all-to-all-start.4 = ((bf16[72,16,288]{2,0,1:T(8,128)(2,1)}), bf16[72,16,288]{2,0,1:T(8,128)(2,1)S(1)}, u32[]{:S(2)}, u32[]{:S(2)}) async-start(bf16[72,16,288]{2,0,1:T(8,128)(2,1)} %copy.28), calls=%async_computation.4 | async-start | bytes 1769472 | tf_op jit(solution)/shard_map/all_to_all | solution.py:594
  14.5 26.5 %copy-start.12 = (bf16[72,4608]{1,0:T(8,128)(2,1)S(1)}, bf16[72,4608]{1,0:T(8,128)(2,1)}, u32[]{:S(2)}) copy-start(bf16[72,4608]{1,0:T(8,128)(2,1)} %param.13) | copy-start | bytes 1990660
  36.8 6.5 %copy-start.2 = (bf16[72,16,288]{2,0,1:T(8,128)(2,1)}, bf16[72,16,288]{2,0,1:T(8,128)(2,1)S(1)}, u32[]{:S(2)}) copy-start(bf16[72,16,288]{2,0,1:T(8,128)(2,1)S(1)} %all-to-all-done.4) | copy-start | bytes 1990660
  36.8 27.7 %all-to-all-start.5 = ((bf16[72,16,288]{2,0,1:T(8,128)(2,1)}), bf16[72,16,288]{2,0,1:T(8,128)(2,1)S(1)}, u32[]{:S(2)}, u32[]{:S(2)}) async-start(bf16[72,16,288]{2,0,1:T(8,128)(2,1)} %copy.29), calls=%async_computation.5 | async-start | bytes 1769472 | tf_op jit(solution)/shard_map/all_to_all | solution.py:594
  42.2 26.5 %copy-start.13 = (bf16[72,4608]{1,0:T(8,128)(2,1)S(1)}, bf16[72,4608]{1,0:T(8,128)(2,1)}, u32[]{:S(2)}) copy-start(bf16[72,4608]{1,0:T(8,128)(2,1)} %param.10) | copy-start | bytes 1990660
  64.5 6.5 %copy-start = (bf16[72,16,288]{2,0,1:T(8,128)(2,1)}, bf16[72,16,288]{2,0,1:T(8,128)(2,1)S(1)}, u32[]{:S(2)}) copy-start(bf16[72,16,288]{2,0,1:T(8,128)(2,1)S(1)} %all-to-all-done.5) | copy-start | bytes 1990660
  64.5 27.7 %all-to-all-start.3 = ((bf16[72,16,288]{2,0,1:T(8,128)(2,1)}), bf16[72,16,288]{2,0,1:T(8,128)(2,1)S(1)}, u32[]{:S(2)}, u32[]{:S(2)}) async-start(bf16[72,16,288]{2,0,1:T(8,128)(2,1)} %copy.27), calls=%async_computation.3 | async-start | bytes 1769472 | tf_op jit(solution)/shard_map/all_to_all | solution.py:594
  69.9 26.5 %copy-start.14 = (bf16[72,4608]{1,0:T(8,128)(2,1)S(1)}, bf16[72,4608]{1,0:T(8,128)(2,1)}, u32[]{:S(2)}) copy-start(bf16[72,4608]{1,0:T(8,128)(2,1)} %param.11) | copy-start | bytes 1990660
  92.1 6.6 %copy-start.4 = (bf16[72,16,288]{2,0,1:T(8,128)(2,1)}, bf16[72,16,288]{2,0,1:T(8,128)(2,1)S(1)}, u32[]{:S(2)}) copy-start(bf16[72,16,288]{2,0,1:T(8,128)(2,1)S(1)} %all-to-all-done.3) | copy-start | bytes 1990660
  92.1 27.7 %all-to-all-start = ((bf16[72,16,288]{2,0,1:T(8,128)(2,1)}), bf16[72,16,288]{2,0,1:T(8,128)(2,1)S(1)}, u32[]{:S(2)}, u32[]{:S(2)}) async-start(bf16[72,16,288]{2,0,1:T(8,128)(2,1)} %copy.24), calls=%async_computation | async-start | bytes 1769472 | tf_op jit(solution)/shard_map/all_to_all | solution.py:594
  97.6 26.5 %copy-start.15 = (bf16[4608,72]{0,1:T(8,128)(2,1)S(1)}, bf16[4608,72]{0,1:T(8,128)(2,1)}, u32[]{:S(2)}) copy-start(bf16[4608,72]{0,1:T(8,128)(2,1)} %param.12) | copy-start | bytes 1990660
  119.8 6.6 %copy-start.7 = (bf16[72,16,288]{2,0,1:T(8,128)(2,1)}, bf16[72,16,288]{2,0,1:T(8,128)(2,1)S(1)}, u32[]{:S(2)}) copy-start(bf16[72,16,288]{2,0,1:T(8,128)(2,1)S(1)} %all-to-all-done) | copy-start | bytes 1990660
  119.8 27.7 %all-to-all-start.1 = ((bf16[72,16,288]{2,0,1:T(8,128)(2,1)}), bf16[72,16,288]{2,0,1:T(8,128)(2,1)S(1)}, u32[]{:S(2)}, u32[]{:S(2)}) async-start(bf16[72,16,288]{2,0,1:T(8,128)(2,1)} %copy.25), calls=%async_computation.1 | async-start | bytes 1769472 | tf_op jit(solution)/shard_map/all_to_all | solution.py:594
  125.2 26.5 %copy-start.10 = (bf16[320,1152]{1,0:T(8,128)(2,1)S(1)}, bf16[320,1152]{1,0:T(8,128)(2,1)}, u32[]{:S(2)}) copy-start(bf16[320,1152]{1,0:T(8,128)(2,1)} %x.1) | copy-start | bytes 2211844
  147.5 27.7 %copy-start.8 = (bf16[72,16,288]{2,0,1:T(8,128)(2,1)}, bf16[72,16,288]{2,0,1:T(8,128)(2,1)S(1)}, u32[]{:S(2)}) copy-start(bf16[72,16,288]{2,0,1:T(8,128)(2,1)S(1)} %all-to-all-done.1) | copy-start | bytes 1990660
  147.5 27.7 %all-to-all-start.2 = ((bf16[72,16,288]{2,0,1:T(8,128)(2,1)}), bf16[72,16,288]{2,0,1:T(8,128)(2,1)S(1)}, u32[]{:S(2)}, u32[]{:S(2)}) async-start(bf16[72,16,288]{2,0,1:T(8,128)(2,1)} %copy.26), calls=%async_computation.2 | async-start | bytes 1769472 | tf_op jit(solution)/shard_map/all_to_all | solution.py:594
  175.2 0.9 copy-start.9
  176.1 179.9 %copy-start.3 = (bf16[72,16,288]{2,0,1:T(8,128)(2,1)S(1)}, bf16[72,16,288]{2,0,1:T(8,128)(2,1)}, u32[]{:S(2)}) copy-start(bf16[72,16,288]{2,0,1:T(8,128)(2,1)} %copy-done.2) | copy-start | bytes 1990660
  176.1 179.9 %copy-start.5 = (bf16[72,16,288]{2,0,1:T(8,128)(2,1)S(1)}, bf16[72,16,288]{2,0,1:T(8,128)(2,1)}, u32[]{:S(2)}) copy-start(bf16[72,16,288]{2,0,1:T(8,128)(2,1)} %copy-done.4) | copy-start | bytes 1990660
  356.0 2.5 copy-start.6
  364.3 1.6 copy-start.1

commit v2 on v1

--- a/solution.py
+++ b/solution.py
@@ -18,6 +18,9 @@
 LO = 640
 LS = 512
 BLK = 144
+NF = 16
+WR = 72
+WL = 256
 ENTRIES = float(3 * D * FF)
 EPS = 1e-06
 SCALE = 2.0**-14
@@ -61,6 +64,8 @@
         self.x = lax.axis_index("dcn")
         fsdp = lax.axis_index("fsdp")
         tp = lax.axis_index("tp")
+        self.f = fsdp
+        self.t = tp
         self.y = fsdp // 4
         self.z = (tp // 2) * 4 + fsdp % 4
         self.c = tp % 2
@@ -81,6 +86,12 @@
     def at_z(self, k):
         return self.dev(z=(self.z + k) % 8)
 
+    def at_f(self, k):
+        return (self.x, (self.f + k) % NF, self.t)
+
+    def across(self, low):
+        return self.dev(z=(1 - self.z // 4) * 4 + low)
+
     def other(self):
         return self.dev(c=1 - self.c)
 
@@ -108,6 +119,59 @@
         copy.start()
         self.sent.append(copy)
         return copy
+
+
+def pack_wide(first, second, wide):
+    for j in range(NF):
+        lanes = slice(j * HB, j * HB + WL)
+        both = jnp.concatenate([first[:, lanes].astype(F32), second[:, lanes].astype(F32)], axis=0)
+        wide[j] = both.astype(BF)
+
+
+def pack_rest(pairs, rest):
+    lane = lax.broadcasted_iota(jnp.int32, (2 * WR, 128), 1)
+    for j in range(NF):
+        start = j * HB + WL
+        base = start - start % 128
+        total = jnp.zeros((2 * WR, 128), F32)
+        for p, (first, second) in enumerate(pairs):
+            both = jnp.concatenate(
+                [first[:, base : base + 128].astype(F32), second[:, base : base + 128].astype(F32)], axis=0
+            )
+            shift = (32 * p - start) % 128
+            if shift:
+                both = pltpu.roll(both, shift, axis=1)
+            total = jnp.where((lane >= 32 * p) & (lane < 32 * p + 32), both, total)
+        rest[j] = total.astype(BF)
+
+
+def unpack(p, wide, rest, first, second):
+    for i in range(NF // 2):
+        rows = slice(i * 2 * WR, (i + 1) * 2 * WR)
+        a, b = wide[2 * i].astype(F32), wide[2 * i + 1].astype(F32)
+        first[rows, 0:WL] = jnp.concatenate([a[:WR], b[:WR]], axis=0).astype(BF)
+        second[rows, 0:WL] = jnp.concatenate([a[WR:], b[WR:]], axis=0).astype(BF)
+        a, b = rest[2 * i].astype(F32), rest[2 * i + 1].astype(F32)
+        if p:
+            a, b = pltpu.roll(a, 128 - 32 * p, axis=1), pltpu.roll(b, 128 - 32 * p, axis=1)
+        first[rows, WL:HB] = jnp.concatenate([a[:WR], b[:WR]], axis=0)[:, 0:32].astype(BF)
+        second[rows, WL:HB] = jnp.concatenate([a[WR:], b[WR:]], axis=0)[:, 0:32].astype(BF)
+
+
+def send_blocks(me, fl, out, land, ssems, rsems, lsem):
+    copies = []
+    for k in range(1, NF):
+        copies.append(
+            fl.start(out.at[(me.f + k) % NF], land.at[me.f], ssems.at[k], rsems.at[k], me.at_f(k))
+        )
+    own = pltpu.make_async_copy(out.at[me.f], land.at[me.f], lsem)
+    own.start()
+    return copies, own
+
+
+def blocks_landed(flight):
+    landed(flight[0])
+    flight[1].wait()
 
 
 def scatter_x(me, fl, stage, slots, sems):
@@ -142,7 +206,7 @@
 class Reduce64:
     def __init__(self, me, fl, n, s):
         self.me, self.fl, self.n = me, fl, n
-        (self.acc, self.send, self.r1, self.t1, self.t1b, self.r2, self.t2, self.t2b, self.r3, self.sems) = s
+        (self.acc, self.send, self.r1, self.t1b, self.r2, self.t2b, self.r3, self.sems) = s
 
     def put(self, index, value):
         self.acc[index] = value
@@ -163,7 +227,6 @@
         self.c1.wait_recv()
         for i in range(self.n):
             total = self.acc[i, :, lanes_of(me.c, LS, LO)] + self.r1[i].astype(F32)
-            self.t1[i] = total
             self.t1b[i] = total.astype(BF)
         self.c2 = []
         for k in (1, 2, 3):
@@ -182,7 +245,8 @@
         me = self.me
         landed(self.c2)
         for i in range(self.n):
-            total = self.t1[i, rows_of(me.y, TQ), :]
+            rows = rows_of(me.y, TQ)
+            total = self.acc[i, rows, lanes_of(me.c, LS, LO)] + self.r1[i, rows, :].astype(F32)
             for k in range(3):
                 total = total + self.r2[k, i].astype(F32)
             self.t2b[i] = total.astype(BF)
@@ -276,10 +340,8 @@
         pltpu.VMEM((n, TOK, DB), F32),
         pltpu.VMEM((n, TOK, DB), BF),
         pltpu.VMEM((n, TOK, LO), BF),
-        pltpu.VMEM((n, TOK, LO), F32),
         pltpu.VMEM((n, TOK, LO), BF),
         pltpu.VMEM((3, n, TQ, LO), BF),
-        pltpu.VMEM((n, TQ, LO), F32),
         pltpu.VMEM((n, TQ, LO), BF),
         pltpu.VMEM((8, n, RQ, LO), BF),
         pltpu.SemaphoreType.DMA((2, 24)),
@@ -336,16 +398,18 @@
 
 
 def kernel(
-    x, x_t, target, w_gate, w_up, w_down, s_gate, s_up, s_down,
-    one, two, scal,
+    x, x_t, target, in_wg, in_wu, in_wd, in_sg, in_su, in_sd,
+    out_g, out_u, out_d, scal,
+    wide_s, wide_r, rest_s, rest_r, sems_w, sems_l,
+    w_gate, w_up, w_down, s_gate, s_up, s_down, one, two,
     kp, kr, kpair, sems_k,
     acc_a, send_a, slots_a, sems_a,
     own, hh, sems_h, mm, sems_m,
-    red_b0, red_b1, red_b2, red_b3, red_b4, red_b5, red_b6, red_b7, red_b8, red_b9,
+    red_b0, red_b1, red_b2, red_b3, red_b4, red_b5, red_b6, red_b7,
     gg,
     acc_c, send_c, slots_c, sems_c,
     gu1, sems_g1, u1d, tan2, h2,
-    red_e0, red_e1, red_e2, red_e3, red_e4, red_e5, red_e6, red_e7, red_e8, red_e9,
+    red_e0, red_e1, red_e2, red_e3, red_e4, red_e5, red_e6, red_e7,
     g2,
     acc_f, send_f, slots_f, sems_f,
     gu2, sems_g2,
@@ -354,29 +418,64 @@
     me = Place()
     fl = Flight()
     starts = (s_gate, s_up, s_down)
+    twos = (out_g, out_u, two)
 
     barrier = pltpu.get_barrier_semaphore()
     peers = (
-        [me.at_x(k) for k in (1, 2, 3)]
-        + [me.at_y(k) for k in (1, 2, 3)]
-        + [me.at_z(k) for k in range(1, 8)]
+        [me.at_f(k) for k in range(1, NF)]
+        + [me.at_x(k) for k in (1, 2, 3)]
+        + [me.across(low) for low in range(4)]
         + [me.other()]
     )
     for peer in peers:
         pl.semaphore_signal(barrier, inc=1, device_id=peer, device_id_type=MESH)
 
-    for i, w in enumerate((w_gate, w_up, s_gate, s_up)):
-        part = nn(x[...], w[...])
-        acc_a[i] = part
-        send_a[i] = part.astype(BF)
-    kp[...] = nt(x[...], x[...])
-    pl.semaphore_wait(barrier, len(peers))
+    pairs = ((in_wg, in_wu), (in_sg, in_su), (in_wd, in_sd))
+    flights = []
+    with jax.named_scope("pack"):
+        pack_wide(*pairs[0], wide_s.at[0])
+    with jax.named_scope("entry"):
+        pl.semaphore_wait(barrier, len(peers))
+    with jax.named_scope("send_blocks"):
+        flights.append(
+            send_blocks(me, fl, wide_s.at[0], wide_r.at[0], sems_w.at[0, 0], sems_w.at[1, 0], sems_l.at[0])
+        )
+        pack_rest(pairs, rest_s)
+        flights.append(send_blocks(me, fl, rest_s, rest_r, sems_w.at[0, 3], sems_w.at[1, 3], sems_l.at[3]))
+        for p in (1, 2):
+            pack_wide(*pairs[p], wide_s.at[p])
+            flights.append(
+                send_blocks(
+                    me, fl, wide_s.at[p], wide_r.at[p], sems_w.at[0, p], sems_w.at[1, p], sems_l.at[p]
+                )
+            )
+    with jax.named_scope("gram"):
+        kp[...] = nt(x[...], x[...])
+        c_k = []
+        for k in (1, 2, 3):
+            c_k.append(fl.start(kp, kr.at[k - 1], sems_k.at[0, k - 1], sems_k.at[1, k - 1], me.at_x(k)))
+
+    def forward(base, first, second):
+        for i, w in enumerate((first, second)):
+            part = nn(x[...], w[...])
+            acc_a[base + i] = part
+            send_a[base + i] = part.astype(BF)
+
+    with jax.named_scope("wait_w"):
+        blocks_landed(flights[0])
+        blocks_landed(flights[1])
+    with jax.named_scope("unpack_w"):
+        unpack(0, wide_r.at[0], rest_r, w_gate, w_up)
+        forward(0, w_gate, w_up)
+    with jax.named_scope("wait_s"):
+        blocks_landed(flights[2])
+    with jax.named_scope("unpack_s"):
+        unpack(1, wide_r.at[1], rest_r, s_gate, s_up)
+        forward(2, s_gate, s_up)
     c_a = scatter_x(me, fl, send_a, slots_a, sems_a)
-    c_k = []
-    for k in (1, 2, 3):
-        c_k.append(fl.start(kp, kr.at[k - 1], sems_k.at[0, k - 1], sems_k.at[1, k - 1], me.at_x(k)))
-
-    landed(c_a)
+
+    with jax.named_scope("wait_a"):
+        landed(c_a)
     my_rows = rows_of(me.x, TQ)
     sums = []
     for i in range(4):
@@ -397,40 +496,52 @@
     own[1] = up_pre * curve
     own[2] = gate_dot
     own[3] = up_dot
-    landed(c_h)
+    with jax.named_scope("wait_h"):
+        landed(c_h)
+    with jax.named_scope("wait_d"):
+        blocks_landed(flights[3])
+    with jax.named_scope("unpack_d"):
+        unpack(2, wide_r.at[2], rest_r, w_down, s_down)
 
     red = Reduce64(
-        me, fl, 2, (red_b0, red_b1, red_b2, red_b3, red_b4, red_b5, red_b6, red_b7, red_b8, red_b9)
-    )
-    red.put(0, nt(hh[0], w_down[...]))
-    red.put(1, nt(hh[1], w_down[...]) + nt(hh[0], s_down[...]))
+        me, fl, 2, (red_b0, red_b1, red_b2, red_b3, red_b4, red_b5, red_b6, red_b7)
+    )
+    with jax.named_scope("out"):
+        red.put(0, nt(hh[0], w_down[...]))
+        red.put(1, nt(hh[1], w_down[...]) + nt(hh[0], s_down[...]))
     red.cores()
-    red.ys()
+    with jax.named_scope("core_sum"):
+        red.ys()
     landed(c_k)
     total = kp[...] + (kr[0] + kr[1] + kr[2])
     high = total.astype(BF)
     kpair[0] = high
     kpair[1] = (total - high.astype(F32)).astype(BF)
-    red.zs()
+    with jax.named_scope("y_sum"):
+        red.zs()
 
     def first_post(i, total, rows, lanes):
         if i == 0:
             total = total - target[rows, lanes].astype(F32)
         return (total / float(TOK)).astype(BF)
 
-    red.finish(gg, first_post)
-
-    part = nn(gg[0], w_down[...])
-    acc_c[0] = part
-    send_c[0] = part.astype(BF)
-    part = nn(gg[1], w_down[...]) + nn(gg[0], s_down[...])
-    acc_c[1] = part
-    send_c[1] = part.astype(BF)
+    with jax.named_scope("z_sum"):
+        red.finish(gg, first_post)
+
+    with jax.named_scope("back"):
+        part = nn(gg[0], w_down[...])
+        acc_c[0] = part
+        send_c[0] = part.astype(BF)
+        part = nn(gg[1], w_down[...]) + nn(gg[0], s_down[...])
+        acc_c[1] = part
+        send_c[1] = part.astype(BF)
     c_c = scatter_x(me, fl, send_c, slots_c, sems_c)
-    part = tn(gg[0], hh[1]) + tn(gg[1], hh[0])
-    one[2] = part
-    u1d[...] = part.astype(BF)
-    landed(c_c)
+    with jax.named_scope("u1d"):
+        part = tn(gg[0], hh[1]) + tn(gg[1], hh[0])
+        one[2] = part
+        u1d[...] = part.astype(BF)
+    with jax.named_scope("wait_c"):
+        landed(c_c)
     sums = []
     for i in range(2):
         total = acc_c[i, my_rows, :]
@@ -447,20 +558,25 @@
     ).astype(BF)
     gu1[1, my_rows, :] = (back_dot * mm[1, my_rows, :] + slope_term * own[2]).astype(BF)
     c_g1 = gather_x(me, fl, gu1, sems_g1)
-    landed(c_m)
-    landed(c_g1)
-
-    for i in range(2):
-        tan2[i] = nn(kpair[0], gu1[i]) + nn(kpair[1], gu1[i])
-    h2[...] = (mm[0] * tan2[0] + mm[1] * tan2[1]).astype(BF)
+    with jax.named_scope("wait_g1"):
+        landed(c_m)
+        landed(c_g1)
+
+    with jax.named_scope("second"):
+        for i in range(2):
+            tan2[i] = nn(kpair[0], gu1[i]) + nn(kpair[1], gu1[i])
+        h2[...] = (mm[0] * tan2[0] + mm[1] * tan2[1]).astype(BF)
     red2 = Reduce64(
-        me, fl, 1, (red_e0, red_e1, red_e2, red_e3, red_e4, red_e5, red_e6, red_e7, red_e8, red_e9)
-    )
-    red2.put(0, nt(h2[...], w_down[...]) + nt(hh[0], u1d[...]))
+        me, fl, 1, (red_e0, red_e1, red_e2, red_e3, red_e4, red_e5, red_e6, red_e7)
+    )
+    with jax.named_scope("out2"):
+        red2.put(0, nt(h2[...], w_down[...]) + nt(hh[0], u1d[...]))
     red2.cores()
-    red2.ys()
-    for i in range(2):
-        one[i] = nn(x_t[...], gu1[i])
+    with jax.named_scope("core_sum2"):
+        red2.ys()
+    with jax.named_scope("image"):
+        for i in range(2):
+            one[i] = nn(x_t[...], gu1[i])
 
     def dots_one(b, carry):
         rows = rows_of(b, BLK)
@@ -474,20 +590,27 @@
         return ss, su, uu
 
     zero = jnp.zeros((8, HB), F32)
-    ss, su, uu = lax.fori_loop(0, DB // BLK, dots_one, (zero, zero, zero))
-    red2.zs()
+    with jax.named_scope("dots"):
+        ss, su, uu = lax.fori_loop(0, DB // BLK, dots_one, (zero, zero, zero))
+    with jax.named_scope("y_sum2"):
+        red2.zs()
     sum1 = ScalarSum(me, fl, sbuf1, ssem1)
-    sum1.go(0, tile_of([whole_sum(ss), whole_sum(su), whole_sum(uu)]))
-    sum1.go(1, sum1.get())
-    red2.finish(g2, lambda i, total, rows, lanes: (total / float(TOK)).astype(BF))
-
-    part = nn(g2[0], w_down[...]) + nn(gg[0], u1d[...])
-    acc_f[0] = part
-    send_f[0] = part.astype(BF)
+    with jax.named_scope("scal"):
+        sum1.go(0, tile_of([whole_sum(ss), whole_sum(su), whole_sum(uu)]))
+        sum1.go(1, sum1.get())
+    with jax.named_scope("z_sum2"):
+        red2.finish(g2, lambda i, total, rows, lanes: (total / float(TOK)).astype(BF))
+
+    with jax.named_scope("back2"):
+        part = nn(g2[0], w_down[...]) + nn(gg[0], u1d[...])
+        acc_f[0] = part
+        send_f[0] = part.astype(BF)
     c_f = scatter_x(me, fl, send_f, slots_f, sems_f)
-    sum1.go(2, sum1.get())
-    two[2] = tn(gg[0], h2[...]) + tn(g2[0], hh[0])
-    landed(c_f)
+    with jax.named_scope("u2d"):
+        sum1.go(2, sum1.get())
+        two[...] = tn(gg[0], h2[...]) + tn(g2[0], hh[0])
+    with jax.named_scope("wait_f"):
+        landed(c_f)
     back_dot = acc_f[0, my_rows, :]
     for k in range(3):
         back_dot = back_dot + slots_f[k, 0].astype(F32)
@@ -498,7 +621,8 @@
     ).astype(BF)
     gu2[1, my_rows, :] = (back_dot * mm[1, my_rows, :] + own[0] * gate_two).astype(BF)
     c_g2 = gather_x(me, fl, gu2, sems_g2)
-    sum1.go(3, sum1.get())
+    with jax.named_scope("scal2"):
+        sum1.go(3, sum1.get())
     norms = sum1.get() * (1.0 / (SCALE * SCALE * ENTRIES))
     s_s, s_u, u_u = norms[0:1, 0:1], norms[1:2, 0:1], norms[2:3, 0:1]
     f = 1.0 / jnp.sqrt(s_s + EPS)
@@ -511,9 +635,11 @@
     v22 = rr / (h21 * h21)
     a1 = f / h21
     a0 = -h11 * f / h21
-    landed(c_g2)
-    for i in range(2):
-        two[i] = nn(x_t[...], gu2[i])
+    with jax.named_scope("wait_g2"):
+        landed(c_g2)
+    with jax.named_scope("image2"):
+        for i in range(2):
+            twos[i][...] = nn(x_t[...], gu2[i])
 
     def dots_two(b, carry):
         rows = rows_of(b, BLK)
@@ -521,7 +647,7 @@
         for i in range(3):
             s = starts[i][rows, :].astype(F32)
             u = one[i, rows, :]
-            w = (a1 * two[i, rows, :] + a0 * u) * SCALE
+            w = (a1 * twos[i][rows, :] + a0 * u) * SCALE
             first = f * s * SCALE
             second = (a1 * u + a0 * s) * SCALE
             p1 = p1 + fold(first * w)
@@ -529,12 +655,14 @@
             pw = pw + fold(w * w)
         return p1, p2, pw
 
-    p1, p2, pw = lax.fori_loop(0, DB // BLK, dots_two, (zero, zero, zero))
+    with jax.named_scope("dots2"):
+        p1, p2, pw = lax.fori_loop(0, DB // BLK, dots_two, (zero, zero, zero))
     sum2 = ScalarSum(me, fl, sbuf2, ssem2)
     tile = tile_of([whole_sum(p1), whole_sum(p2), whole_sum(pw)])
-    for stage in range(4):
-        sum2.go(stage, tile)
-        tile = sum2.get()
+    with jax.named_scope("scal3"):
+        for stage in range(4):
+            sum2.go(stage, tile)
+            tile = sum2.get()
     norms = tile * (1.0 / (SCALE * SCALE * ENTRIES))
     h12, h22, ww = norms[0:1, 0:1], norms[1:2, 0:1], norms[2:3, 0:1]
     rr = (
@@ -548,7 +676,19 @@
     c2 = a1 / h32
     c1 = (a0 - h22 * a1) / h32
     c0 = -(h12 * f + h22 * a0) / h32
-    scal[...] = tile_of([h21, h12, h22, h32, h11, c2, c1, c0])
+    scal[...] = tile_of([h21, h12, h22, h32, h11])
+    with jax.named_scope("third"):
+        for i, out in enumerate((out_g, out_u)):
+            def third(b, carry, i=i, out=out):
+                rows = rows_of(b, BLK)
+                out[rows, :] = c2 * twos[i][rows, :] + c1 * one[i, rows, :] + c0 * starts[i][rows, :].astype(F32)
+                return carry
+
+            lax.fori_loop(0, DB // BLK, third, 0)
+        for b in range(DB // 128):
+            rows = slice(b * 128, (b + 1) * 128)
+            value = c2 * two[rows, :] + c1 * one[2, rows, :] + c0 * s_down[rows, :].astype(F32)
+            out_d[:, rows] = value.T
 
     for copy in fl.sent:
         copy.wait_send()
@@ -559,7 +699,12 @@
 def rounds(*operands):
     dma = pltpu.SemaphoreType.DMA
     scratch = (
-        [pltpu.VMEM((TOK, TOK), F32), pltpu.VMEM((3, TOK, TOK), F32), pltpu.VMEM((2, TOK, TOK), BF), dma((2, 3))]
+        [pltpu.VMEM((3, NF, 2 * WR, WL), BF)] * 2
+        + [pltpu.VMEM((NF, 2 * WR, 128), BF)] * 2
+        + [dma((2, 4, NF)), dma((4,))]
+        + [pltpu.VMEM((DB, HB), BF)] * 6
+        + [pltpu.VMEM((3, DB, HB), F32), pltpu.VMEM((DB, HB), F32)]
+        + [pltpu.VMEM((TOK, TOK), F32), pltpu.VMEM((3, TOK, TOK), F32), pltpu.VMEM((2, TOK, TOK), BF), dma((2, 3))]
         + [pltpu.VMEM((4, TOK, HB), F32), pltpu.VMEM((4, TOK, HB), BF), pltpu.VMEM((3, 4, TQ, HB), BF), dma((2, 3))]
         + [pltpu.VMEM((4, TQ, HB), F32), pltpu.VMEM((2, TOK, HB), BF), dma((2, 3)), pltpu.VMEM((2, TOK, HB), F32), dma((2, 3))]
         + reduce_scratch(2)
@@ -575,38 +720,29 @@
     return pl.pallas_call(
         kernel,
         out_shape=(
-            jax.ShapeDtypeStruct((3, DB, HB), F32),
-            jax.ShapeDtypeStruct((3, DB, HB), F32),
+            jax.ShapeDtypeStruct((DB, HB), F32),
+            jax.ShapeDtypeStruct((DB, HB), F32),
+            jax.ShapeDtypeStruct((HB, DB), F32),
             jax.ShapeDtypeStruct((8, 128), F32),
         ),
         in_specs=[pl.BlockSpec(memory_space=pltpu.VMEM)] * 9,
-        out_specs=[pl.BlockSpec(memory_space=pltpu.VMEM)] * 3,
+        out_specs=[pl.BlockSpec(memory_space=pltpu.VMEM)] * 4,
         scratch_shapes=scratch,
         compiler_params=pltpu.CompilerParams(
-            collective_id=0, has_side_effects=True, vmem_limit_bytes=58 * 1024 * 1024
+            collective_id=0, has_side_effects=True, vmem_limit_bytes=60 * 1024 * 1024
         ),
         name="arnoldi",
     )(*operands)
 
 
 def on_device(inputs, target, w_gate, w_up, w_down, start_gate, start_up, start_down):
-    def regroup(w):
-        return lax.all_to_all(w, "fsdp", split_axis=1, concat_axis=0, tiled=True)
-
-    gate_cols, up_cols, start_gcols, start_ucols = map(regroup, (w_gate, w_up, start_gate, start_up))
-    down_cols, start_dcols = map(regroup, (w_down.T, start_down.T))
-    one, two, scal = rounds(
-        inputs, inputs.T, target, gate_cols, up_cols, down_cols, start_gcols, start_ucols, start_dcols
-    )
-    c2, c1, c0 = scal[5, 0], scal[6, 0], scal[7, 0]
-    third = [
-        c2 * two[i] + c1 * one[i] + c0 * s.astype(F32)
-        for i, s in enumerate((start_gcols, start_ucols, start_dcols))
-    ]
+    third_g, third_u, third_d, scal = rounds(
+        inputs, inputs.T, target, w_gate, w_up, w_down.T, start_gate, start_up, start_down.T
+    )
     return (
-        third[0].reshape(DB, 1, HB),
-        third[1].reshape(DB, 1, HB),
-        third[2].T.reshape(1, HB, DB),
+        third_g.reshape(DB, 1, HB),
+        third_u.reshape(DB, 1, HB),
+        third_d.reshape(1, HB, DB),
         scal[0:4, 0],
         scal[4:5, 0],
     )

time: 374 us -> 256 us (0.68)
  waiting for transfers between devices: 128 us -> 0 us
  Pallas kernels: 177 us -> 244 us
  starting transfers between devices: 30.1 us -> 0 us
  local copies, waits for them, and re-layouts: 26.2 us -> 10.5 us
  other arithmetic: 9.64 us -> 0 us
    all_to_all x6 -> x0, waiting for transfers between devices: 128 us -> none  [regroup(): return lax.all_to_all(w, 'fsdp', split_axis=1, concat_axis=0, tiled=True)]
    pallas_call x1, Pallas kernels: 177 us -> 244 us  [rounds(): pl.pallas_call(kernel, out_shape=(jax.ShapeDtypeStruct((DB, HB), F32), ja...]
    all_to_all x6 -> x0, starting transfers between devices: 30.1 us -> none  [regroup(): return lax.all_to_all(w, 'fsdp', split_axis=1, concat_axis=0, tiled=True)]
    all_to_all x12 -> x0, local copies, waits for them, and re-layouts: 15 us -> none  [regroup(): return lax.all_to_all(w, 'fsdp', split_axis=1, concat_axis=0, tiled=True)]
    reshape x1 -> x0, other arithmetic: 4.35 us -> none  [on_device(): third[2].T.reshape(1, HB, DB)]
    add x1 -> x0, other arithmetic: 4.23 us -> none  [on_device(): c2 * two[i] + c1 * one[i] + c0 * s.astype(F32)]
    unnamed x36 -> x8, local copies, waits for them, and re-layouts: 8.45 us -> 8.01 us
  transfers between devices with their start and end apart: 6 -> 0, of which waited for: 6 -> 0; matrix products, arithmetic and copies ran while one was open for 2% -> 0% of each run, Pallas kernels for 0% -> 0%
where the time goes in v2:
time: 256 us; the launch traced here: 255 us
  Pallas kernels  244 us (95%)
  local copies, waits for them, and re-layouts  10.5 us (4%)
    pallas_call x1, Pallas kernels, rounds(): pl.pallas_call(kernel, out_shape=(jax.ShapeDtypeStruct((DB, HB), F32), ja...  244 us
    unnamed x8, local copies, waits for them, and re-layouts  8.01 us

profile of v2, /device:TPU:1, one launch (start us, length us, event | category | flops | bytes accessed | tf_op | source)
XLA Modules:
  0.0 254.9 jit_solution(4856973428256782460)
XLA Ops:
  0.6 2.2 copy.16
  2.8 243.7 %arnoldi.1 = (f32[1152,288]{1,0:T(8,128)}, f32[1152,288]{1,0:T(8,128)}, f32[288,1152]{1,0:T(8,128)}, f32[8,128]{1,0:T(8,128)}) custom-call(bf16[320,1152]{1,0:T(8,128)(2,1)} %x.1, bf16[1152,320]{1,0:T(8,128)(2,1)} %bitcast.7, bf16[320,1152]{1,0:T(8,128)(2,1)} %target.1, bf16[72,4608]{1,0:T(8,128)(2,1)} %in_wg.1, bf16[72,4608]{1,0:T(8,128)(2,1)} %in_wu.1, ...), custom_call_target="tpu_custom_call" | custom-call | tf_op jit(solution)/shard_map/arnoldi/pallas_call | solution.py:720
  246.6 1.2 slice.7
  247.8 1.3 slice_reduce_fusion
  249.1 0.0 copy-start
  249.1 3.2 %copy.17 = f32[1152,1,288]{0,2,1:T(8,128)} copy(f32[1152,1,288]{2,0,1:T(8,128)} %bitcast.9) | data formatting | bytes 2654208
  252.2 0.0 copy-done
  252.2 0.0 copy-start.1
  252.2 1.6 copy.18
  253.8 0.0 copy-done.1
  253.8 1.1 copy.20
Async XLA Ops:
  249.1 3.2 %copy-start = (f32[1152,288]{1,0:T(8,128)S(1)}, f32[1152,288]{1,0:T(8,128)}, u32[]{:S(2)}) copy-start(f32[1152,288]{1,0:T(8,128)} %get-tuple-element.10) | copy-start | bytes 3981316
  252.2 1.6 copy-start.1

commit v3 on v2

v3 whole, which is shorter than its diff:
```python
import math

import jax
import jax.numpy as jnp
from jax import lax
from jax.experimental import pallas as pl
from jax.experimental.pallas import tpu as pltpu
from jax.sharding import PartitionSpec as P

D = 4608
FF = 18432
TOK = 320
DB = 1152
HB = 288
TQ = 80
RQ = 16
NRED = 5
BLK = 48
NF = 16
WR = 72
WL = 256
ENTRIES = float(3 * D * FF)
EPS = 1e-06
SCALE = 2.0**-14
MESH = pl.DeviceIdType.MESH
BF = jnp.bfloat16
F32 = jnp.float32

gelu_cubic = 0.044715
gelu_scale = math.sqrt(2.0 / math.pi)


def gelu_parts(argument):
    squared = argument * argument
    inner_arg = gelu_scale * (argument + gelu_cubic * squared * argument)
    tanh_val = jnp.tanh(inner_arg)
    sech_square = 1.0 - tanh_val * tanh_val
    inner_slope = gelu_scale * (1.0 + 3.0 * gelu_cubic * squared)
    inner_curve = gelu_scale * 6.0 * gelu_cubic * argument
    gelu_val = 0.5 * argument * (1.0 + tanh_val)
    gelu_slope = 0.5 * (1.0 + tanh_val) + 0.5 * argument * sech_square * inner_slope
    gelu_curve = sech_square * inner_slope + 0.5 * argument * (
        sech_square * inner_curve - 2.0 * tanh_val * sech_square * inner_slope * inner_slope
    )
    return (gelu_val, gelu_slope, gelu_curve)


def nn(a, b):
    return lax.dot_general(a, b, (((1,), (0,)), ((), ())), preferred_element_type=F32)


def nt(a, b):
    return lax.dot_general(a, b, (((1,), (1,)), ((), ())), preferred_element_type=F32)


def tn(a, b):
    return lax.dot_general(a, b, (((0,), (0,)), ((), ())), preferred_element_type=F32)


class Place:
    def __init__(self):
        self.x = lax.axis_index("dcn")
        fsdp = lax.axis_index("fsdp")
        tp = lax.axis_index("tp")
        self.f = fsdp
        self.t = tp
        self.y = fsdp // 4
        self.z = (tp // 2) * 4 + fsdp % 4
        self.c = tp % 2

    def dev(self, x=None, y=None, z=None, c=None):
        x = self.x if x is None else x
        y = self.y if y is None else y
        z = self.z if z is None else z
        c = self.c if c is None else c
        return (x, y * 4 + z % 4, (z // 4) * 2 + c)

    def at_x(self, k):
        return self.dev(x=(self.x + k) % 4)

    def at_y(self, k):
        return self.dev(y=(self.y + k) % 4)

    def at_z(self, k):
        return self.dev(z=(self.z + k) % 8)

    def at_f(self, k):
        return (self.x, (self.f + k) % NF, self.t)

    def at_t(self, k):
        return (self.x, self.f, (self.t + k) % 4)

    def across(self, low):
        return self.dev(z=(1 - self.z // 4) * 4 + low)

    def other(self):
        return self.dev(c=1 - self.c)


def rows_of(index, size):
    return pl.ds(pl.multiple_of(index * size, size), size)


def lanes_at(start, size):
    return pl.ds(pl.multiple_of(start, 128), size)


def remote(src, dst, ssem, rsem, dev):
    return pltpu.make_async_remote_copy(
        src_ref=src, dst_ref=dst, send_sem=ssem, recv_sem=rsem, device_id=dev, device_id_type=MESH
    )


class Flight:
    def __init__(self):
        self.sent = []

    def start(self, src, dst, ssem, rsem, dev):
        copy = remote(src, dst, ssem, rsem, dev)
        copy.start()
        self.sent.append(copy)
        return copy


def pack_wide(first, second, wide):
    for j in range(NF):
        lanes = slice(j * HB, j * HB + WL)
        both = jnp.concatenate([first[:, lanes].astype(F32), second[:, lanes].astype(F32)], axis=0)
        wide[j] = both.astype(BF)


def pack_rest(pairs, rest):
    lane = lax.broadcasted_iota(jnp.int32, (2 * WR, 128), 1)
    for j in range(NF):
        start = j * HB + WL
        base = start - start % 128
        total = jnp.zeros((2 * WR, 128), F32)
        for p, (first, second) in enumerate(pairs):
            both = jnp.concatenate(
                [first[:, base : base + 128].astype(F32), second[:, base : base + 128].astype(F32)], axis=0
            )
            shift = (32 * p - start) % 128
            if shift:
                both = pltpu.roll(both, shift, axis=1)
            total = jnp.where((lane >= 32 * p) & (lane < 32 * p + 32), both, total)
        rest[j] = total.astype(BF)


def unpack(p, wide, rest, first, second):
    for i in range(NF // 2):
        rows = slice(i * 2 * WR, (i + 1) * 2 * WR)
        a, b = wide[2 * i].astype(F32), wide[2 * i + 1].astype(F32)
        first[rows, 0:WL] = jnp.concatenate([a[:WR], b[:WR]], axis=0).astype(BF)
        second[rows, 0:WL] = jnp.concatenate([a[WR:], b[WR:]], axis=0).astype(BF)
        a, b = rest[2 * i].astype(F32), rest[2 * i + 1].astype(F32)
        if p:
            a, b = pltpu.roll(a, 128 - 32 * p, axis=1), pltpu.roll(b, 128 - 32 * p, axis=1)
        first[rows, WL:HB] = jnp.concatenate([a[:WR], b[:WR]], axis=0)[:, 0:32].astype(BF)
        second[rows, WL:HB] = jnp.concatenate([a[WR:], b[WR:]], axis=0)[:, 0:32].astype(BF)


def send_blocks(me, fl, out, land, ssems, rsems, lsem):
    copies = []
    for k in range(1, NF):
        copies.append(
            fl.start(out.at[(me.f + k) % NF], land.at[me.f], ssems.at[k], rsems.at[k], me.at_f(k))
        )
    own = pltpu.make_async_copy(out.at[me.f], land.at[me.f], lsem)
    own.start()
    return copies, own


def blocks_landed(flight):
    landed(flight[0])
    flight[1].wait()


def scatter_x(me, fl, stage, slots, sems):
    out = []
    for k in (1, 2, 3):
        peer = (me.x + k) % 4
        out.append(
            fl.start(
                stage.at[:, rows_of(peer, TQ), :],
                slots.at[k - 1],
                sems.at[0, k - 1],
                sems.at[1, k - 1],
                me.at_x(k),
            )
        )
    return out


def gather_x(me, fl, buf, sems):
    out = []
    mine = buf.at[:, rows_of(me.x, TQ), :]
    for k in (1, 2, 3):
        out.append(fl.start(mine, mine, sems.at[0, k - 1], sems.at[1, k - 1], me.at_x(k)))
    return out


def landed(copies):
    for copy in copies:
        copy.wait_recv()


class Chunk:
    def __init__(self, me, fl, acc, send, scratch, low, width, back, back_width):
        self.me, self.fl, self.acc, self.send = me, fl, acc, send
        (self.r1, self.t1b, self.r2, self.t2b, self.r3, self.sems) = scratch
        self.mine = lanes_at(low(me.c), width)
        self.theirs = lanes_at(low(1 - me.c), width)
        self.back = lanes_at(back(me.c), back_width)

    def go(self, src, dst, sem, dev, rsem=None):
        return self.fl.start(src, dst, self.sems.at[0, sem], self.sems.at[1, sem], dev)

    def put(self, value):
        self.acc[...] = value
        self.send[...] = value.astype(BF)

    def cores(self):
        me = self.me
        self.c1 = {}
        for k in (1, 2, 3, 0):
            rows = rows_of((me.y + k) % 4, TQ)
            self.c1[k] = self.go(self.send.at[rows, self.theirs], self.r1.at[rows, :], k, me.other())

    def ys(self):
        me = self.me
        self.c2 = []
        for k in (1, 2, 3):
            landed([self.c1[k]])
            rows = rows_of((me.y + k) % 4, TQ)
            self.t1b[rows, :] = (self.acc[rows, self.mine] + self.r1[rows, :].astype(F32)).astype(BF)
            self.c2.append(self.go(self.t1b.at[rows, :], self.r2.at[k - 1], 3 + k, me.at_y(k)))

    def zs(self):
        me = self.me
        landed([self.c1[0]])
        rows = rows_of(me.y, TQ)
        total = self.acc[rows, self.mine] + self.r1[rows, :].astype(F32)
        landed(self.c2)
        for k in range(3):
            total = total + self.r2[k].astype(F32)
        self.t2b[...] = total.astype(BF)
        for q in range(NRED):

            @pl.when(me.z != q)
            def _():
                remote(
                    self.t2b.at[q * RQ : (q + 1) * RQ, :],
                    self.r3.at[me.z],
                    self.sems.at[0, 7 + q],
                    self.sems.at[1, 7 + me.z],
                    me.dev(z=q),
                ).start()

    def reduce(self, final, post):
        me = self.me
        self.final = final

        @pl.when(me.z < NRED)
        def _():
            self.r3[me.z] = self.t2b[rows_of(me.z, RQ), :]
            for s in range(8):

                @pl.when(me.z != s)
                def _():
                    remote(
                        self.t2b.at[0:RQ, :],
                        self.r3.at[s],
                        self.sems.at[0, 7],
                        self.sems.at[1, 7 + s],
                        me.other(),
                    ).wait_recv()

            rows = pl.ds(pl.multiple_of(me.y * TQ + me.z * RQ, RQ), RQ)
            total = self.r3[0].astype(F32)
            for s in range(1, 8):
                total = total + self.r3[s].astype(F32)
            final[rows, self.mine] = post(total, rows, self.mine)
            for k in range(1, 8):
                piece = final.at[rows, self.mine]
                remote(
                    piece, piece, self.sems.at[0, 14 + k], self.sems.at[1, 15 + me.z], me.at_z(k)
                ).start()

    def spread(self):
        me, final = self.me, self.final
        for q in range(NRED):
            piece = final.at[pl.ds(pl.multiple_of(me.y * TQ + q * RQ, RQ), RQ), self.mine]

            @pl.when(me.z != q)
            def _():
                remote(piece, piece, self.sems.at[0, 7], self.sems.at[1, 15 + q], me.other()).wait_recv()

        rows = rows_of(me.y, TQ)
        block = final.at[rows, self.mine]
        self.c5 = [self.go(block, block, 21 + k, me.at_y(k)) for k in (1, 2, 3)]
        block = final.at[rows, self.back]
        self.c6 = [self.go(block, block, 25, me.other())]

    def collect(self):
        me, final = self.me, self.final
        for k in (1, 2, 3):
            landed([self.c5[k - 1]])
            block = final.at[rows_of((me.y + 4 - k) % 4, TQ), self.back]
            self.c6.append(self.go(block, block, 25 + k, me.other()))
        landed(self.c6)

    def drain(self):
        me = self.me
        for q in range(NRED):

            @pl.when(me.z != q)
            def _():
                remote(
                    self.t2b.at[q * RQ : (q + 1) * RQ, :],
                    self.r3.at[me.z],
                    self.sems.at[0, 7 + q],
                    self.sems.at[1, 7 + me.z],
                    me.dev(z=q),
                ).wait_send()

        @pl.when(me.z < NRED)
        def _():
            for k in range(1, 8):
                remote(
                    self.t2b.at[0:RQ, :],
                    self.t2b.at[0:RQ, :],
                    self.sems.at[0, 14 + k],
                    self.sems.at[1, 15],
                    me.other(),
                ).wait_send()


def chunk_scratch(width):
    return [
        pltpu.VMEM((TOK, width), BF),
        pltpu.VMEM((TOK, width), BF),
        pltpu.VMEM((3, TQ, width), BF),
        pltpu.VMEM((TQ, width), BF),
        pltpu.VMEM((8, RQ, width), BF),
        pltpu.SemaphoreType.DMA((2, 30)),
    ]


class ScalarSum:
    def __init__(self, me, fl, buf, sems):
        self.me, self.fl, self.buf, self.sems = me, fl, buf, sems

    def go(self, stage, tile):
        me = self.me
        index, base, count, at = (
            (me.x, 0, 4, me.at_x),
            (me.f, 4, 16, me.at_f),
            (me.t, 20, 4, me.at_t),
        )[stage]
        mine = self.buf.at[base + index]
        self.buf[base + index] = tile
        self.copies = []
        for k in range(1, count):
            self.copies.append(
                self.fl.start(mine, mine, self.sems.at[0, base + k], self.sems.at[1, base + k], at(k))
            )
        self.span = (base, count)

    def get(self):
        landed(self.copies)
        base, count = self.span
        total = self.buf[base]
        for s in range(1, count):
            total = total + self.buf[base + s]
        return total


def whole_sum(value):
    return jnp.sum(jnp.sum(value, axis=1, keepdims=True), axis=0, keepdims=True)


def fold(value):
    return jnp.sum(value.reshape(BLK // 8, 8, DB), axis=0)


def tile_of(values):
    rows = [jnp.broadcast_to(v, (1, 128)) for v in values]
    while len(rows) < 8:
        rows.append(jnp.zeros((1, 128), F32))
    return jnp.concatenate(rows, axis=0)


def add_x(acc, slots, rows, i):
    total = acc[i, rows, :]
    for k in range(3):
        total = total + slots[k, i].astype(F32)
    return total


def whole_low(c):
    return c * 512


def whole_back(c):
    return c * 640


def outer_low(c):
    return c * 768


def inner_low(c):
    return 384 + c * 128


def inner_back(c):
    return 384 + c * 256


def kernel(
    x, target, in_wg, in_wu, in_wd, in_sg, in_su, in_sd,
    out_g, out_u, out_d, hess, ray,
    wide_s, wide_r, rest_s, rest_r, sems_w, sems_l,
    w_gate, w_up, w_down, s_gate, s_up, s_down, start_t, one,
    kp, kr, kpair, sems_k,
    acc_a, send_a, slots_a, sems_a, acc_d, send_d, slots_d, sems_d,
    own, hh, sems_h, mm, sems_m,
    acc_o, send_o, acc_p, send_p,
    o0, o1, o2, o3, o4, o5, p0, p1, p2, p3, p4, p5,
    go, gd,
    acc_b, send_b, slots_b, sems_b, acc_c, send_c, slots_c, sems_c,
    gu1, sems_g1, u1d, tan2, h2,
    q0, q1, q2, q3, q4, q5, r0, r1, r2, r3, r4, r5,
    g2,
    acc_f, send_f, slots_f, sems_f,
    gu2, sems_g2,
    sbuf1, ssem1, sbuf2, ssem2,
):
    me = Place()
    fl = Flight()
    twos = (out_g, out_u, out_d)

    barrier = pltpu.get_barrier_semaphore()
    peers = (
        [me.at_f(k) for k in range(1, NF)]
        + [me.at_t(k) for k in (1, 2, 3)]
        + [me.at_x(k) for k in (1, 2, 3)]
        + [me.across(low) for low in range(4)]
    )
    for peer in peers:
        pl.semaphore_signal(barrier, inc=1, device_id=peer, device_id_type=MESH)

    pairs = ((in_wg, in_wu), (in_sg, in_su), (in_wd, in_sd))
    flights = []

    def send_wide(p):
        flights.append(
            send_blocks(me, fl, wide_s.at[p], wide_r.at[p], sems_w.at[0, p], sems_w.at[1, p], sems_l.at[p])
        )

    with jax.named_scope("regroup"):
        pack_wide(*pairs[0], wide_s.at[0])
        pl.semaphore_wait(barrier, len(peers))
        send_wide(0)
        pack_rest(pairs, rest_s)
        flights.append(send_blocks(me, fl, rest_s, rest_r, sems_w.at[0, 3], sems_w.at[1, 3], sems_l.at[3]))
        pack_wide(*pairs[1], wide_s.at[1])
        send_wide(1)
        pack_wide(*pairs[2], wide_s.at[2])
    with jax.named_scope("gram"):
        kp[...] = nt(x[...], x[...])
        c_k = []
        for k in (1, 2, 3):
            c_k.append(fl.start(kp, kr.at[k - 1], sems_k.at[0, k - 1], sems_k.at[1, k - 1], me.at_x(k)))

    def partial(acc, send, i, value):
        acc[i] = value
        send[i] = value.astype(BF)

    with jax.named_scope("forward"):
        blocks_landed(flights[0])
        blocks_landed(flights[1])
        send_wide(2)
        unpack(0, wide_r.at[0], rest_r, w_gate, w_up)
        for i, w in enumerate((w_gate, w_up)):
            partial(acc_a, send_a, i, nn(x[...], w[...]))
        c_a = scatter_x(me, fl, send_a, slots_a, sems_a)
        blocks_landed(flights[2])
        unpack(1, wide_r.at[1], rest_r, s_gate, s_up)
        for i, w in enumerate((s_gate, s_up)):
            partial(acc_d, send_d, i, nn(x[...], w[...]))
        c_d = scatter_x(me, fl, send_d, slots_d, sems_d)
    my_rows = rows_of(me.x, TQ)
    with jax.named_scope("hidden"):
        landed(c_a)
        gate_pre, up_pre = add_x(acc_a, slots_a, my_rows, 0), add_x(acc_a, slots_a, my_rows, 1)
        val, slope, curve = gelu_parts(gate_pre)
        slope_up = slope * up_pre
        hh[0, my_rows, :] = (val * up_pre).astype(BF)
        mm[0, my_rows, :] = slope_up
        mm[1, my_rows, :] = val
        own[0] = slope
        own[1] = up_pre * curve
        landed(c_d)
        gate_dot, up_dot = add_x(acc_d, slots_d, my_rows, 0), add_x(acc_d, slots_d, my_rows, 1)
        hh[1, my_rows, :] = (mm[0, my_rows, :] * gate_dot + mm[1, my_rows, :] * up_dot).astype(BF)
        c_h = gather_x(me, fl, hh, sems_h)
        own[2] = gate_dot
        own[3] = up_dot

    def transposed(i, s):
        for b in range(DB // 128):
            cols = slice(b * 128, (b + 1) * 128)
            start_t[i, :, cols] = s[cols, :].astype(F32).T.astype(BF)

    with jax.named_scope("starts"):
        transposed(0, s_gate)
        transposed(1, s_up)
        landed(c_k)
        total = kp[...] + (kr[0] + kr[1] + kr[2])
        high = total.astype(BF)
        kpair[0] = high
        kpair[1] = (total - high.astype(F32)).astype(BF)
        landed(c_h)
        c_m = gather_x(me, fl, mm, sems_m)
        blocks_landed(flights[3])
        unpack(2, wide_r.at[2], rest_r, w_down, s_down)

    def out_post(total, rows, lanes):
        return ((total - target[rows, lanes].astype(F32)) / float(TOK)).astype(BF)

    def dot_post(total, rows, lanes):
        return (total / float(TOK)).astype(BF)

    def both(first, second, posts, finals, second_partial):
        first.cores()
        second_partial()
        second.cores()
        first.ys()
        second.ys()
        first.zs()
        second.zs()
        first.reduce(finals[0], posts[0])
        second.reduce(finals[1], posts[1])
        first.spread()
        second.spread()
        first.collect()

    ch_o = Chunk(me, fl, acc_o, send_o, (o0, o1, o2, o3, o4, o5), whole_low, 640, whole_back, 512)
    ch_p = Chunk(me, fl, acc_p, send_p, (p0, p1, p2, p3, p4, p5), whole_low, 640, whole_back, 512)
    with jax.named_scope("outputs"):
        ch_o.put(nt(hh[0], w_down[...]))
        both(
            ch_o,
            ch_p,
            (out_post, dot_post),
            (go, gd),
            lambda: ch_p.put(nt(hh[1], w_down[...]) + nt(hh[0], s_down[...])),
        )
    with jax.named_scope("back"):
        partial(acc_b, send_b, 0, nn(go[...], w_down[...]))
        c_b = scatter_x(me, fl, send_b, slots_b, sems_b)
        ch_p.collect()
        partial(acc_c, send_c, 0, nn(gd[...], w_down[...]) + nn(go[...], s_down[...]))
        c_c = scatter_x(me, fl, send_c, slots_c, sems_c)
        image = tn(hh[1], go[...]) + tn(hh[0], gd[...])
        one[2] = image
        u1d[...] = image.astype(BF)
        transposed(2, s_down)
        landed(c_b)
        grad_hidden = add_x(acc_b, slots_b, my_rows, 0)
        own[0] = grad_hidden * own[0]
        own[1] = grad_hidden * own[1]
        landed(c_c)
        back_dot = add_x(acc_c, slots_c, my_rows, 0)
        slope_term, curve_term = own[0], own[1]
        gu1[0, my_rows, :] = (
            back_dot * mm[0, my_rows, :] + slope_term * own[3] + curve_term * own[2]
        ).astype(BF)
        gu1[1, my_rows, :] = (back_dot * mm[1, my_rows, :] + slope_term * own[2]).astype(BF)
        c_g1 = gather_x(me, fl, gu1, sems_g1)
        landed(c_m)
        landed(c_g1)

    with jax.named_scope("second"):
        for i in range(2):
            tan2[i] = nn(kpair[0], gu1[i]) + nn(kpair[1], gu1[i])
        h2[...] = (mm[0] * tan2[0] + mm[1] * tan2[1]).astype(BF)
        ch_q = Chunk(me, fl, acc_o, send_o, (q0, q1, q2, q3, q4, q5), outer_low, 384, outer_low, 384)
        ch_r = Chunk(me, fl, acc_o, send_o, (r0, r1, r2, r3, r4, r5), inner_low, 256, inner_back, 128)
        for copy in ch_o.c1.values():
            copy.wait_send()
        done = [id(copy) for copy in ch_o.c1.values()]
        fl.sent = [copy for copy in fl.sent if id(copy) not in done]
        ch_q.put(nt(h2[...], w_down[...]) + nn(hh[0], u1d[...]))
        ch_q.cores()
        ch_r.cores()
        ch_q.ys()
        ch_r.ys()

    def dots_one(b, carry):
        rows = rows_of(b, BLK)
        ss, su, uu = carry
        for i in range(3):
            s = start_t[i, rows, :].astype(F32) * SCALE
            u = one[i, rows, :] * SCALE
            ss = ss + fold(s * s)
            su = su + fold(s * u)
            uu = uu + fold(u * u)
        return ss, su, uu

    zero = jnp.zeros((8, DB), F32)
    sum1 = ScalarSum(me, fl, sbuf1, ssem1)
    with jax.named_scope("image"):
        one[0] = tn(gu1[0], x[...])
        one[1] = tn(gu1[1], x[...])
        ch_q.zs()
        ch_r.zs()
        ss, su, uu = lax.fori_loop(0, HB // BLK, dots_one, (zero, zero, zero))
        ch_q.reduce(g2, dot_post)
        ch_r.reduce(g2, dot_post)
        sum1.go(0, tile_of([whole_sum(ss), whole_sum(su), whole_sum(uu)]))
        ch_q.spread()
        ch_r.spread()
        sum1.go(1, sum1.get())
        ch_q.collect()
        ch_r.collect()

    with jax.named_scope("back_second"):
        partial(acc_f, send_f, 0, nn(g2[...], w_down[...]) + nt(go[...], u1d[...]))
        c_f = scatter_x(me, fl, send_f, slots_f, sems_f)
        out_d[...] = tn(h2[...], go[...]) + tn(hh[0], g2[...])
        sum1.go(2, sum1.get())
        landed(c_f)
        back_dot = add_x(acc_f, slots_f, my_rows, 0)
        gate_two = tan2[0, my_rows, :]
        up_two = tan2[1, my_rows, :]
        gu2[0, my_rows, :] = (
            back_dot * mm[0, my_rows, :] + own[0] * up_two + own[1] * gate_two
        ).astype(BF)
        gu2[1, my_rows, :] = (back_dot * mm[1, my_rows, :] + own[0] * gate_two).astype(BF)
        c_g2 = gather_x(me, fl, gu2, sems_g2)
        norms = sum1.get() * (1.0 / (SCALE * SCALE * ENTRIES))
    s_s, s_u, u_u = norms[0:1, 0:1], norms[1:2, 0:1], norms[2:3, 0:1]
    f = 1.0 / jnp.sqrt(s_s + EPS)
    v11 = f * f * s_s
    h11 = f * f * s_u
    w11 = f * f * u_u
    rr = jnp.maximum(w11 - h11 * h11 * (2.0 - v11), 0.0)
    h21 = jnp.sqrt(rr + EPS)
    v12 = (h11 - h11 * v11) / h21
    v22 = rr / (h21 * h21)
    a1 = f / h21
    a0 = -h11 * f / h21

    def dots_two(b, carry):
        rows = rows_of(b, BLK)
        p1, p2, pw = carry
        s = start_t[2, rows, :].astype(F32)
        u = one[2, rows, :]
        w = (a1 * out_d[rows, :] + a0 * u) * SCALE
        first = f * s * SCALE
        second = (a1 * u + a0 * s) * SCALE
        return p1 + fold(first * w), p2 + fold(second * w), pw + fold(w * w)

    with jax.named_scope("last_dots"):
        d1, d2, dw = lax.fori_loop(0, HB // BLK, dots_two, (zero, zero, zero))
        d1, d2, dw = whole_sum(d1), whole_sum(d2), whole_sum(dw)
        for i in range(2):
            w = (
                a1 * gu2[i, my_rows, :].astype(F32) + a0 * gu1[i, my_rows, :].astype(F32)
            ) * SCALE
            first = own[2 + i]
            second = a1 * tan2[i, my_rows, :] + a0 * first
            d1 = d1 + whole_sum((f * SCALE) * first * w)
            d2 = d2 + whole_sum(second * SCALE * w)
        sum2 = ScalarSum(me, fl, sbuf2, ssem2)
        sum2.go(0, tile_of([d1, d2, dw]))
        landed(c_g2)
        dw = jnp.zeros((1, 1), F32)
        for i in range(2):
            w = (a1 * gu2[i].astype(F32) + a0 * gu1[i].astype(F32)) * SCALE
            high = w.astype(BF)
            low = (w - high.astype(F32)).astype(BF)
            kw = nn(kpair[0], high) + nn(kpair[1], high) + nn(kpair[0], low)
            dw = dw + whole_sum(w * kw)
        blank = jnp.zeros((1, 1), F32)
        sum2.go(1, sum2.get() + tile_of([blank, blank, dw]))
        out_g[...] = tn(gu2[0], x[...])
        sum2.go(2, sum2.get())
        out_u[...] = tn(gu2[1], x[...])
        norms = sum2.get() * (1.0 / (SCALE * SCALE * ENTRIES))
    h12, h22, ww = norms[0:1, 0:1], norms[1:2, 0:1], norms[2:3, 0:1]
    rr = (
        ww
        - 2.0 * (h12 * h12 + h22 * h22)
        + h12 * h12 * v11
        + h22 * h22 * v22
        + 2.0 * h12 * h22 * v12
    )
    h32 = jnp.sqrt(jnp.maximum(rr, 0.0) + EPS)
    c2 = a1 / h32
    c1 = (a0 - h22 * a1) / h32
    c0 = -(h12 * f + h22 * a0) / h32
    for i, value in enumerate((h21, h12, h22, h32)):
        hess[i] = jnp.max(value)
    ray[0] = jnp.max(h11)

    def third(b, carry):
        rows = rows_of(b, BLK)
        for i in range(3):
            twos[i][rows, :] = (
                c2 * twos[i][rows, :] + c1 * one[i, rows, :] + c0 * start_t[i, rows, :].astype(F32)
            )
        return carry

    with jax.named_scope("third"):
        lax.fori_loop(0, HB // BLK, third, 0)

    for copy in fl.sent:
        copy.wait_send()
    for chunk in (ch_o, ch_p, ch_q, ch_r):
        chunk.drain()


def rounds(*operands):
    dma = pltpu.SemaphoreType.DMA

    def xround(n):
        return [pltpu.VMEM((n, TOK, HB), F32), pltpu.VMEM((n, TOK, HB), BF), pltpu.VMEM((3, n, TQ, HB), BF), dma((2, 3))]

    scratch = (
        [pltpu.VMEM((3, NF, 2 * WR, WL), BF)] * 2
        + [pltpu.VMEM((NF, 2 * WR, 128), BF)] * 2
        + [dma((2, 4, NF)), dma((4,))]
        + [pltpu.VMEM((DB, HB), BF)] * 6
        + [pltpu.VMEM((3, HB, DB), BF), pltpu.VMEM((3, HB, DB), F32)]
        + [pltpu.VMEM((TOK, TOK), F32), pltpu.VMEM((3, TOK, TOK), F32), pltpu.VMEM((2, TOK, TOK), BF), dma((2, 3))]
        + xround(2) + xround(2)
        + [pltpu.VMEM((4, TQ, HB), F32), pltpu.VMEM((2, TOK, HB), BF), dma((2, 3)), pltpu.VMEM((2, TOK, HB), F32), dma((2, 3))]
        + [pltpu.VMEM((TOK, DB), F32), pltpu.VMEM((TOK, DB), BF)] * 2
        + chunk_scratch(640) + chunk_scratch(640)
        + [pltpu.VMEM((TOK, DB), BF)] * 2
        + xround(1) + xround(1)
        + [pltpu.VMEM((2, TOK, HB), BF), dma((2, 3)), pltpu.VMEM((HB, DB), BF), pltpu.VMEM((2, TOK, HB), F32), pltpu.VMEM((TOK, HB), BF)]
        + chunk_scratch(384) + chunk_scratch(256)
        + [pltpu.VMEM((TOK, DB), BF)]
        + xround(1)
        + [pltpu.VMEM((2, TOK, HB), BF), dma((2, 3))]
        + [pltpu.VMEM((24, 8, 128), F32), dma((2, 24)), pltpu.VMEM((24, 8, 128), F32), dma((2, 24))]
    )
    wide = jax.ShapeDtypeStruct((HB, DB), F32)
    return pl.pallas_call(
        kernel,
        out_shape=(wide, wide, wide, jax.ShapeDtypeStruct((4,), F32), jax.ShapeDtypeStruct((1,), F32)),
        in_specs=[pl.BlockSpec(memory_space=pltpu.VMEM)] * 8,
        out_specs=[pl.BlockSpec(memory_space=pltpu.VMEM)] * 3 + [pl.BlockSpec(memory_space=pltpu.SMEM)] * 2,
        scratch_shapes=scratch,
        compiler_params=pltpu.CompilerParams(
            collective_id=0, has_side_effects=True, vmem_limit_bytes=60 * 1024 * 1024
        ),
        name="arnoldi",
    )(*operands)


def on_device(inputs, target, w_gate, w_up, w_down, start_gate, start_up, start_down):
    third_g, third_u, third_d, hess, ray = rounds(
        inputs, target, w_gate, w_up, w_down.T, start_gate, start_up, start_down.T
    )
    return (
        third_g.T.reshape(DB, 1, HB),
        third_u.T.reshape(DB, 1, HB),
        third_d.reshape(1, HB, DB),
        hess,
        ray,
    )


def solution(mesh):
    placed = (
        P(None, "dcn"),
        P(None, "dcn"),
        P(("dcn", "fsdp"), "tp"),
        P(("dcn", "fsdp"), "tp"),
        P("tp", ("dcn", "fsdp")),
        P(("dcn", "fsdp"), "tp"),
        P(("dcn", "fsdp"), "tp"),
        P("tp", ("dcn", "fsdp")),
    )
    return jax.shard_map(
        on_device,
        mesh=mesh,
        in_specs=placed,
        out_specs=(
            P("dcn", "tp", "fsdp"),
            P("dcn", "tp", "fsdp"),
            P("tp", "fsdp", "dcn"),
            P(),
            P(),
        ),
        check_vma=False,
    )
```

time: 256 us -> 227 us (0.89)
  Pallas kernels: 244 us -> 218 us
  local copies, waits for them, and re-layouts: 10.5 us -> 5.96 us
    pallas_call x1, Pallas kernels: 244 us -> 218 us  [rounds(): pl.pallas_call(kernel, out_shape=(wide, wide, wide, jax.ShapeDtypeStruct(...]
    unnamed x8 -> x10, local copies, waits for them, and re-layouts: 8.01 us -> 5.96 us
where the time goes in v3:
time: 227 us; the launch traced here: 226 us
  Pallas kernels  218 us (96%)
  local copies, waits for them, and re-layouts  5.96 us (3%)
  between operations  2.42 us (1%)
    pallas_call x1, Pallas kernels, rounds(): pl.pallas_call(kernel, out_shape=(wide, wide, wide, jax.ShapeDtypeStruct(...  218 us
    unnamed x10, local copies, waits for them, and re-layouts  5.96 us

profile of v3, /device:TPU:1, one launch (start us, length us, event | category | flops | bytes accessed | tf_op | source)
XLA Modules:
  0.0 226.5 jit_solution(8509735595191295741)
XLA Ops:
  0.6 218.1 %arnoldi.1 = (f32[288,1152]{1,0:T(8,128)}, f32[288,1152]{1,0:T(8,128)}, f32[288,1152]{1,0:T(8,128)}, f32[4]{0:T(128)}, f32[1]{0:T(128)}) custom-call(bf16[320,1152]{1,0:T(8,128)(2,1)} %x.1, bf16[320,1152]{1,0:T(8,128)(2,1)} %target.1, bf16[72,4608]{1,0:T(8,128)(2,1)} %in_wg.1, bf16[72,4608]{1,0:T(8,128)(2,1)} %in_wu.1, bf16[72,4608]{1,0:T(8,128)(2,1)} %bitcast.12, ...), custom_call_target="tpu_custom_call" | custom-call | tf_op jit(solution)/shard_map/arnoldi/pallas_call | solution.py:753
  218.7 0.0 copy-start.1
  218.8 2.6 %copy.18 = f32[1152,1,288]{0,2,1:T(8,128)} copy(f32[1152,1,288]{0,2,1:T(8,128)} %bitcast.11) | data formatting | bytes 2654208
  221.3 0.0 copy-done.1
  221.3 0.0 copy-start
  221.3 1.1 copy.19
  222.4 0.7 copy-done
  223.1 0.0 copy-start.2
  223.1 1.1 copy.20
  224.2 0.0 copy-done.2
  224.2 0.5 copy.21
Async XLA Ops:
  218.7 2.6 %copy-start.1 = (f32[288,1152]{1,0:T(8,128)S(1)}, f32[288,1152]{1,0:T(8,128)}, u32[]{:S(2)}) copy-start(f32[288,1152]{1,0:T(8,128)} %get-tuple-element.11) | copy-start | bytes 3981316
  221.3 1.8 copy-start
  223.1 1.1 copy-start.2

commit v4 on v3

--- a/solution.py
+++ b/solution.py
@@ -19,6 +19,8 @@
 NF = 16
 WR = 72
 WL = 256
+SR = 24
+BR = 176
 ENTRIES = float(3 * D * FF)
 EPS = 1e-06
 SCALE = 2.0**-14
@@ -65,6 +67,9 @@
         self.f = fsdp
         self.t = tp
         self.y = fsdp // 4
+        self.half = (fsdp % 4) // 2
+        self.m = self.y * 2 + fsdp % 2
+        self.p = fsdp + 2 - 4 * self.half
         self.z = (tp // 2) * 4 + fsdp % 4
         self.c = tp % 2
 
@@ -87,6 +92,14 @@
     def at_f(self, k):
         return (self.x, (self.f + k) % NF, self.t)
 
+    def near(self, k):
+        m = (self.m + k) % 8
+        f = (m // 2) * 4 + self.half * 2 + m % 2
+        return f, f + 2 - 4 * self.half
+
+    def partner(self):
+        return (self.x, self.p, self.t)
+
     def at_t(self, k):
         return (self.x, self.f, (self.t + k) % 4)
 
@@ -122,57 +135,89 @@
         return copy
 
 
-def pack_wide(first, second, wide):
+def pack(first, second, out):
+    lane = lax.broadcasted_iota(jnp.int32, (SR, 128), 1)
     for j in range(NF):
         lanes = slice(j * HB, j * HB + WL)
-        both = jnp.concatenate([first[:, lanes].astype(F32), second[:, lanes].astype(F32)], axis=0)
-        wide[j] = both.astype(BF)
-
-
-def pack_rest(pairs, rest):
-    lane = lax.broadcasted_iota(jnp.int32, (2 * WR, 128), 1)
-    for j in range(NF):
+        wide = jnp.concatenate([first[:, lanes].astype(F32), second[:, lanes].astype(F32)], axis=0)
         start = j * HB + WL
         base = start - start % 128
-        total = jnp.zeros((2 * WR, 128), F32)
-        for p, (first, second) in enumerate(pairs):
-            both = jnp.concatenate(
-                [first[:, base : base + 128].astype(F32), second[:, base : base + 128].astype(F32)], axis=0
-            )
-            shift = (32 * p - start) % 128
-            if shift:
-                both = pltpu.roll(both, shift, axis=1)
-            total = jnp.where((lane >= 32 * p) & (lane < 32 * p + 32), both, total)
-        rest[j] = total.astype(BF)
-
-
-def unpack(p, wide, rest, first, second):
-    for i in range(NF // 2):
-        rows = slice(i * 2 * WR, (i + 1) * 2 * WR)
-        a, b = wide[2 * i].astype(F32), wide[2 * i + 1].astype(F32)
-        first[rows, 0:WL] = jnp.concatenate([a[:WR], b[:WR]], axis=0).astype(BF)
-        second[rows, 0:WL] = jnp.concatenate([a[WR:], b[WR:]], axis=0).astype(BF)
-        a, b = rest[2 * i].astype(F32), rest[2 * i + 1].astype(F32)
-        if p:
-            a, b = pltpu.roll(a, 128 - 32 * p, axis=1), pltpu.roll(b, 128 - 32 * p, axis=1)
-        first[rows, WL:HB] = jnp.concatenate([a[:WR], b[:WR]], axis=0)[:, 0:32].astype(BF)
-        second[rows, WL:HB] = jnp.concatenate([a[WR:], b[WR:]], axis=0)[:, 0:32].astype(BF)
-
-
-def send_blocks(me, fl, out, land, ssems, rsems, lsem):
+        both = jnp.concatenate(
+            [first[:, base : base + 128].astype(F32), second[:, base : base + 128].astype(F32)], axis=0
+        )
+        tiles = []
+        for group in ((0, 1, 2, 3), (4, 5)):
+            tile = jnp.zeros((SR, 128), F32)
+            for g in group:
+                strip = both[g * SR : (g + 1) * SR]
+                at = (32 * g) % 128
+                shift = (at - start) % 128
+                if shift:
+                    strip = pltpu.roll(strip, shift, axis=1)
+                tile = jnp.where((lane >= at) & (lane < at + 32), strip, tile)
+            tiles.append(tile)
+        rest = jnp.concatenate(tiles, axis=1)
+        blank = jnp.zeros((BR - 2 * WR - SR, WL), F32)
+        out[j] = jnp.concatenate([wide, rest, blank], axis=0).astype(BF)
+
+
+def unpack(a, b, first, second, rows):
+    a, b = a[...].astype(F32), b[...].astype(F32)
+    rests = []
+    for v in (a, b):
+        strips = []
+        for g in range(6):
+            at = 32 * g
+            tile = v[2 * WR : 2 * WR + SR, at - at % 128 : at - at % 128 + 128]
+            if at % 128:
+                tile = pltpu.roll(tile, 128 - at % 128, axis=1)
+            strips.append(tile)
+        rests.append(jnp.concatenate(strips, axis=0))
+    first[rows, 0:WL] = jnp.concatenate([a[:WR], b[:WR]], axis=0).astype(BF)
+    second[rows, 0:WL] = jnp.concatenate([a[WR : 2 * WR], b[WR : 2 * WR]], axis=0).astype(BF)
+    a, b = rests
+    first[rows, WL:HB] = jnp.concatenate([a[:WR], b[:WR]], axis=0)[:, 0:32].astype(BF)
+    second[rows, WL:HB] = jnp.concatenate([a[WR:], b[WR:]], axis=0)[:, 0:32].astype(BF)
+
+
+def unpack_half(half, blocks, first, second):
+    for y in range(4):
+        rows = pl.ds(pl.multiple_of(y * 4 * WR + half * 2 * WR, 2 * WR), 2 * WR)
+        unpack(blocks.at[2 * y], blocks.at[2 * y + 1], first, second, rows)
+
+
+def send_blocks(me, fl, out, land, sems, lsem):
     copies = []
     for k in range(1, NF):
         copies.append(
-            fl.start(out.at[(me.f + k) % NF], land.at[me.f], ssems.at[k], rsems.at[k], me.at_f(k))
+            fl.start(out.at[(me.f + k) % NF], land.at[me.f], sems.at[0, k], sems.at[1, k], me.at_f(k))
         )
     own = pltpu.make_async_copy(out.at[me.f], land.at[me.f], lsem)
     own.start()
+    return copies, (own,)
+
+
+def send_near(me, fl, out, land, sems, lsems):
+    copies = []
+    for k in range(1, 8):
+        f, p = me.near(k)
+        for q, j in enumerate((f, p)):
+            copies.append(
+                fl.start(
+                    out.at[j], land.at[q, me.m], sems.at[0, q, k], sems.at[1, q, k], (me.x, f, me.t)
+                )
+            )
+    own = []
+    for q, j in enumerate((me.f, me.p)):
+        own.append(pltpu.make_async_copy(out.at[j], land.at[q, me.m], lsems.at[q]))
+        own[-1].start()
     return copies, own
 
 
 def blocks_landed(flight):
     landed(flight[0])
-    flight[1].wait()
+    for copy in flight[1]:
+        copy.wait()
 
 
 def scatter_x(me, fl, stage, slots, sems):
@@ -390,8 +435,8 @@
     return jnp.concatenate(rows, axis=0)
 
 
-def add_x(acc, slots, rows, i):
-    total = acc[i, rows, :]
+def add_x(send, slots, rows, i):
+    total = send[i, rows, :].astype(F32)
     for k in range(3):
         total = total + slots[k, i].astype(F32)
     return total
@@ -420,19 +465,19 @@
 def kernel(
     x, target, in_wg, in_wu, in_wd, in_sg, in_su, in_sd,
     out_g, out_u, out_d, hess, ray,
-    wide_s, wide_r, rest_s, rest_r, sems_w, sems_l,
-    w_gate, w_up, w_down, s_gate, s_up, s_down, start_t, one,
+    out_w, near_r, full_r, far_r, sems_w, sems_n, sems_l, sems_p,
+    parts, w_down, s_down, start_t, one, cross_s, cross_r,
     kp, kr, kpair, sems_k,
-    acc_a, send_a, slots_a, sems_a, acc_d, send_d, slots_d, sems_d,
+    send_a, slots_a, sems_a, send_d, slots_d, sems_d,
     own, hh, sems_h, mm, sems_m,
     acc_o, send_o, acc_p, send_p,
     o0, o1, o2, o3, o4, o5, p0, p1, p2, p3, p4, p5,
     go, gd,
-    acc_b, send_b, slots_b, sems_b, acc_c, send_c, slots_c, sems_c,
+    send_b, slots_b, sems_b, send_c, slots_c, sems_c,
     gu1, sems_g1, u1d, tan2, h2,
     q0, q1, q2, q3, q4, q5, r0, r1, r2, r3, r4, r5,
     g2,
-    acc_f, send_f, slots_f, sems_f,
+    send_f, slots_f, sems_f,
     gu2, sems_g2,
     sbuf1, ssem1, sbuf2, ssem2,
 ):
@@ -453,47 +498,61 @@
     pairs = ((in_wg, in_wu), (in_sg, in_su), (in_wd, in_sd))
     flights = []
 
-    def send_wide(p):
-        flights.append(
-            send_blocks(me, fl, wide_s.at[p], wide_r.at[p], sems_w.at[0, p], sems_w.at[1, p], sems_l.at[p])
-        )
-
     with jax.named_scope("regroup"):
-        pack_wide(*pairs[0], wide_s.at[0])
+        pack(*pairs[0], out_w.at[0])
         pl.semaphore_wait(barrier, len(peers))
-        send_wide(0)
-        pack_rest(pairs, rest_s)
-        flights.append(send_blocks(me, fl, rest_s, rest_r, sems_w.at[0, 3], sems_w.at[1, 3], sems_l.at[3]))
-        pack_wide(*pairs[1], wide_s.at[1])
-        send_wide(1)
-        pack_wide(*pairs[2], wide_s.at[2])
+        flights.append(send_near(me, fl, out_w.at[0], near_r.at[0], sems_n.at[0], sems_l.at[0]))
+        pack(*pairs[1], out_w.at[1])
+        flights.append(send_near(me, fl, out_w.at[1], near_r.at[1], sems_n.at[1], sems_l.at[1]))
+        pack(*pairs[2], out_w.at[2])
+        parts[...] = jnp.zeros(parts.shape, BF)
+
+    def squares(b, total):
+        rows = pl.ds(pl.multiple_of(b * 8, 8), 8)
+        for ref in (in_sg, in_su, in_sd):
+            v = ref[rows, :].astype(F32) * SCALE
+            total = total + v * v
+        return total
+
     with jax.named_scope("gram"):
         kp[...] = nt(x[...], x[...])
         c_k = []
         for k in (1, 2, 3):
             c_k.append(fl.start(kp, kr.at[k - 1], sems_k.at[0, k - 1], sems_k.at[1, k - 1], me.at_x(k)))
-
-    def partial(acc, send, i, value):
-        acc[i] = value
+        start_square = lax.fori_loop(0, WR // 8, squares, jnp.zeros((8, FF // 4), F32))
+        start_square = whole_sum(start_square)
+
+    def partial(send, i, value):
         send[i] = value.astype(BF)
+
+    my_rows = rows_of(me.x, TQ)
+
+    def forward(p, send, slots, sems):
+        for q in range(2):
+            unpack_half(me.half, near_r.at[p, q], parts.at[q, 2 * p], parts.at[q, 2 * p + 1])
+            for i in range(2):
+                partial(send, 2 * q + i, nn(x[...], parts[q, 2 * p + i]))
+        return scatter_x(me, fl, send, slots, sems)
+
+    def cross(p, send, slots):
+        for i in range(2):
+            cross_s[p, i] = add_x(send, slots, my_rows, 2 + i).astype(BF)
+        return fl.start(cross_s.at[p], cross_r.at[p], sems_p.at[0, p], sems_p.at[1, p], me.partner())
+
+    def joined(p, send, slots, i):
+        return add_x(send, slots, my_rows, i) + cross_r[p, i].astype(F32)
 
     with jax.named_scope("forward"):
         blocks_landed(flights[0])
+        flights.append(send_blocks(me, fl, out_w.at[2], full_r, sems_w, sems_l.at[2, 0]))
+        c_a = forward(0, send_a, slots_a, sems_a)
         blocks_landed(flights[1])
-        send_wide(2)
-        unpack(0, wide_r.at[0], rest_r, w_gate, w_up)
-        for i, w in enumerate((w_gate, w_up)):
-            partial(acc_a, send_a, i, nn(x[...], w[...]))
-        c_a = scatter_x(me, fl, send_a, slots_a, sems_a)
-        blocks_landed(flights[2])
-        unpack(1, wide_r.at[1], rest_r, s_gate, s_up)
-        for i, w in enumerate((s_gate, s_up)):
-            partial(acc_d, send_d, i, nn(x[...], w[...]))
-        c_d = scatter_x(me, fl, send_d, slots_d, sems_d)
-    my_rows = rows_of(me.x, TQ)
+        c_d = forward(1, send_d, slots_d, sems_d)
+        landed(c_a)
+        cross_a = cross(0, send_a, slots_a)
     with jax.named_scope("hidden"):
-        landed(c_a)
-        gate_pre, up_pre = add_x(acc_a, slots_a, my_rows, 0), add_x(acc_a, slots_a, my_rows, 1)
+        landed([cross_a])
+        gate_pre, up_pre = joined(0, send_a, slots_a, 0), joined(0, send_a, slots_a, 1)
         val, slope, curve = gelu_parts(gate_pre)
         slope_up = slope * up_pre
         hh[0, my_rows, :] = (val * up_pre).astype(BF)
@@ -502,7 +561,9 @@
         own[0] = slope
         own[1] = up_pre * curve
         landed(c_d)
-        gate_dot, up_dot = add_x(acc_d, slots_d, my_rows, 0), add_x(acc_d, slots_d, my_rows, 1)
+        cross_d = cross(1, send_d, slots_d)
+        landed([cross_d])
+        gate_dot, up_dot = joined(1, send_d, slots_d, 0), joined(1, send_d, slots_d, 1)
         hh[1, my_rows, :] = (mm[0, my_rows, :] * gate_dot + mm[1, my_rows, :] * up_dot).astype(BF)
         c_h = gather_x(me, fl, hh, sems_h)
         own[2] = gate_dot
@@ -514,17 +575,18 @@
             start_t[i, :, cols] = s[cols, :].astype(F32).T.astype(BF)
 
     with jax.named_scope("starts"):
-        transposed(0, s_gate)
-        transposed(1, s_up)
-        landed(c_k)
-        total = kp[...] + (kr[0] + kr[1] + kr[2])
-        high = total.astype(BF)
-        kpair[0] = high
-        kpair[1] = (total - high.astype(F32)).astype(BF)
         landed(c_h)
         c_m = gather_x(me, fl, mm, sems_m)
-        blocks_landed(flights[3])
-        unpack(2, wide_r.at[2], rest_r, w_down, s_down)
+        blocks_landed(flights[2])
+        for i in range(NF // 2):
+            rows = slice(i * 2 * WR, (i + 1) * 2 * WR)
+            unpack(full_r.at[2 * i], full_r.at[2 * i + 1], w_down, s_down, rows)
+
+    def far(part):
+        blocks = pl.ds(part * 4, 4)
+        return fl.start(
+            near_r.at[1, 1, blocks], far_r.at[blocks], sems_p.at[0, 2 + part], sems_p.at[1, 2 + part], me.partner()
+        )
 
     def out_post(total, rows, lanes):
         return ((total - target[rows, lanes].astype(F32)) / float(TOK)).astype(BF)
@@ -558,21 +620,22 @@
             lambda: ch_p.put(nt(hh[1], w_down[...]) + nt(hh[0], s_down[...])),
         )
     with jax.named_scope("back"):
-        partial(acc_b, send_b, 0, nn(go[...], w_down[...]))
+        partial(send_b, 0, nn(go[...], w_down[...]))
         c_b = scatter_x(me, fl, send_b, slots_b, sems_b)
+        c_far = [far(0)]
         ch_p.collect()
-        partial(acc_c, send_c, 0, nn(gd[...], w_down[...]) + nn(go[...], s_down[...]))
+        partial(send_c, 0, nn(gd[...], w_down[...]) + nn(go[...], s_down[...]))
         c_c = scatter_x(me, fl, send_c, slots_c, sems_c)
         image = tn(hh[1], go[...]) + tn(hh[0], gd[...])
         one[2] = image
         u1d[...] = image.astype(BF)
         transposed(2, s_down)
         landed(c_b)
-        grad_hidden = add_x(acc_b, slots_b, my_rows, 0)
+        grad_hidden = add_x(send_b, slots_b, my_rows, 0)
         own[0] = grad_hidden * own[0]
         own[1] = grad_hidden * own[1]
         landed(c_c)
-        back_dot = add_x(acc_c, slots_c, my_rows, 0)
+        back_dot = add_x(send_c, slots_c, my_rows, 0)
         slope_term, curve_term = own[0], own[1]
         gu1[0, my_rows, :] = (
             back_dot * mm[0, my_rows, :] + slope_term * own[3] + curve_term * own[2]
@@ -580,6 +643,11 @@
         gu1[1, my_rows, :] = (back_dot * mm[1, my_rows, :] + slope_term * own[2]).astype(BF)
         c_g1 = gather_x(me, fl, gu1, sems_g1)
         landed(c_m)
+        landed(c_k)
+        total = kp[...] + (kr[0] + kr[1] + kr[2])
+        high = total.astype(BF)
+        kpair[0] = high
+        kpair[1] = (total - high.astype(F32)).astype(BF)
         landed(c_g1)
 
     with jax.named_scope("second"):
@@ -600,14 +668,10 @@
 
     def dots_one(b, carry):
         rows = rows_of(b, BLK)
-        ss, su, uu = carry
-        for i in range(3):
-            s = start_t[i, rows, :].astype(F32) * SCALE
-            u = one[i, rows, :] * SCALE
-            ss = ss + fold(s * s)
-            su = su + fold(s * u)
-            uu = uu + fold(u * u)
-        return ss, su, uu
+        su, uu = carry
+        s = start_t[2, rows, :].astype(F32) * SCALE
+        u = one[2, rows, :] * SCALE
+        return su + fold(s * u), uu + fold(u * u)
 
     zero = jnp.zeros((8, DB), F32)
     sum1 = ScalarSum(me, fl, sbuf1, ssem1)
@@ -616,10 +680,15 @@
         one[1] = tn(gu1[1], x[...])
         ch_q.zs()
         ch_r.zs()
-        ss, su, uu = lax.fori_loop(0, HB // BLK, dots_one, (zero, zero, zero))
+        su, uu = lax.fori_loop(0, HB // BLK, dots_one, (zero, zero))
+        su, uu = whole_sum(su), whole_sum(uu)
+        for i in range(2):
+            g = gu1[i, my_rows, :].astype(F32) * SCALE
+            su = su + whole_sum(own[2 + i] * SCALE * g)
+            uu = uu + whole_sum(tan2[i, my_rows, :] * SCALE * g)
         ch_q.reduce(g2, dot_post)
         ch_r.reduce(g2, dot_post)
-        sum1.go(0, tile_of([whole_sum(ss), whole_sum(su), whole_sum(uu)]))
+        sum1.go(0, tile_of([start_square, su, uu]))
         ch_q.spread()
         ch_r.spread()
         sum1.go(1, sum1.get())
@@ -627,12 +696,13 @@
         ch_r.collect()
 
     with jax.named_scope("back_second"):
-        partial(acc_f, send_f, 0, nn(g2[...], w_down[...]) + nt(go[...], u1d[...]))
+        partial(send_f, 0, nn(g2[...], w_down[...]) + nt(go[...], u1d[...]))
         c_f = scatter_x(me, fl, send_f, slots_f, sems_f)
+        c_far.append(far(1))
         out_d[...] = tn(h2[...], go[...]) + tn(hh[0], g2[...])
         sum1.go(2, sum1.get())
         landed(c_f)
-        back_dot = add_x(acc_f, slots_f, my_rows, 0)
+        back_dot = add_x(send_f, slots_f, my_rows, 0)
         gate_two = tan2[0, my_rows, :]
         up_two = tan2[1, my_rows, :]
         gu2[0, my_rows, :] = (
@@ -689,6 +759,10 @@
         out_g[...] = tn(gu2[0], x[...])
         sum2.go(2, sum2.get())
         out_u[...] = tn(gu2[1], x[...])
+        landed(c_far)
+        unpack_half(1 - me.half, far_r, parts.at[0, 2], parts.at[0, 3])
+        transposed(0, parts.at[0, 2])
+        transposed(1, parts.at[0, 3])
         norms = sum2.get() * (1.0 / (SCALE * SCALE * ENTRIES))
     h12, h22, ww = norms[0:1, 0:1], norms[1:2, 0:1], norms[2:3, 0:1]
     rr = (
@@ -727,16 +801,15 @@
     dma = pltpu.SemaphoreType.DMA
 
     def xround(n):
-        return [pltpu.VMEM((n, TOK, HB), F32), pltpu.VMEM((n, TOK, HB), BF), pltpu.VMEM((3, n, TQ, HB), BF), dma((2, 3))]
+        return [pltpu.VMEM((n, TOK, HB), BF), pltpu.VMEM((3, n, TQ, HB), BF), dma((2, 3))]
 
     scratch = (
-        [pltpu.VMEM((3, NF, 2 * WR, WL), BF)] * 2
-        + [pltpu.VMEM((NF, 2 * WR, 128), BF)] * 2
-        + [dma((2, 4, NF)), dma((4,))]
-        + [pltpu.VMEM((DB, HB), BF)] * 6
-        + [pltpu.VMEM((3, HB, DB), BF), pltpu.VMEM((3, HB, DB), F32)]
+        [pltpu.VMEM((3, NF, BR, WL), BF), pltpu.VMEM((2, 2, 8, BR, WL), BF), pltpu.VMEM((NF, BR, WL), BF), pltpu.VMEM((8, BR, WL), BF)]
+        + [dma((2, NF)), dma((2, 2, 2, 8)), dma((3, 2)), dma((2, 4))]
+        + [pltpu.VMEM((2, 4, DB, HB), BF)] + [pltpu.VMEM((DB, HB), BF)] * 2
+        + [pltpu.VMEM((3, HB, DB), BF), pltpu.VMEM((3, HB, DB), F32)] + [pltpu.VMEM((2, 2, TQ, HB), BF)] * 2
         + [pltpu.VMEM((TOK, TOK), F32), pltpu.VMEM((3, TOK, TOK), F32), pltpu.VMEM((2, TOK, TOK), BF), dma((2, 3))]
-        + xround(2) + xround(2)
+        + xround(4) + xround(4)
         + [pltpu.VMEM((4, TQ, HB), F32), pltpu.VMEM((2, TOK, HB), BF), dma((2, 3)), pltpu.VMEM((2, TOK, HB), F32), dma((2, 3))]
         + [pltpu.VMEM((TOK, DB), F32), pltpu.VMEM((TOK, DB), BF)] * 2
         + chunk_scratch(640) + chunk_scratch(640)

time: 227 us -> 207 us (0.912)
  Pallas kernels: 218 us -> 199 us
    pallas_call x1, Pallas kernels: 218 us -> 199 us  [rounds(): pl.pallas_call(kernel, out_shape=(wide, wide, wide, jax.ShapeDtypeStruct(...]
where the time goes in v4:
time: 207 us
  Pallas kernels  199 us (96%)
  local copies, waits for them, and re-layouts  5.96 us (3%)
  between operations  2.42 us (1%)
    pallas_call x1, Pallas kernels, rounds(): pl.pallas_call(kernel, out_shape=(wide, wide, wide, jax.ShapeDtypeStruct(...  199 us
    unnamed x10, local copies, waits for them, and re-layouts  5.96 us

profile of v4, /device:TPU:1, one launch (start us, length us, event | category | flops | bytes accessed | tf_op | source)
XLA Modules:
  0.0 207.2 jit_solution(8923024468061634966)
XLA Ops:
  0.6 198.8 %arnoldi.1 = (f32[288,1152]{1,0:T(8,128)}, f32[288,1152]{1,0:T(8,128)}, f32[288,1152]{1,0:T(8,128)}, f32[4]{0:T(128)}, f32[1]{0:T(128)}) custom-call(bf16[320,1152]{1,0:T(8,128)(2,1)} %x.1, bf16[320,1152]{1,0:T(8,128)(2,1)} %target.1, bf16[72,4608]{1,0:T(8,128)(2,1)} %in_wg.1, bf16[72,4608]{1,0:T(8,128)(2,1)} %in_wu.1, bf16[72,4608]{1,0:T(8,128)(2,1)} %bitcast.12, ...), custom_call_target="tpu_custom_call" | custom-call | tf_op jit(solution)/shard_map/arnoldi/pallas_call | solution.py:826
  199.4 0.0 copy-start.1
  199.5 2.6 %copy.18 = f32[1152,1,288]{0,2,1:T(8,128)} copy(f32[1152,1,288]{0,2,1:T(8,128)} %bitcast.11) | data formatting | bytes 2654208
  202.0 0.0 copy-done.1
  202.0 0.0 copy-start
  202.0 1.1 copy.19
  203.1 0.7 copy-done
  203.8 0.0 copy-start.2
  203.8 1.1 copy.20
  204.9 0.0 copy-done.2
  204.9 0.5 copy.21
Async XLA Ops:
  199.4 2.6 %copy-start.1 = (f32[288,1152]{1,0:T(8,128)S(1)}, f32[288,1152]{1,0:T(8,128)}, u32[]{:S(2)}) copy-start(f32[288,1152]{1,0:T(8,128)} %get-tuple-element.11) | copy-start | bytes 3981316
  202.0 1.8 copy-start
  203.8 1.1 copy-start.2

commit v5 on v4

--- a/solution.py
+++ b/solution.py
@@ -527,12 +527,11 @@
 
     my_rows = rows_of(me.x, TQ)
 
-    def forward(p, send, slots, sems):
+    def products(p, send):
         for q in range(2):
             unpack_half(me.half, near_r.at[p, q], parts.at[q, 2 * p], parts.at[q, 2 * p + 1])
             for i in range(2):
                 partial(send, 2 * q + i, nn(x[...], parts[q, 2 * p + i]))
-        return scatter_x(me, fl, send, slots, sems)
 
     def cross(p, send, slots):
         for i in range(2):
@@ -545,29 +544,26 @@
     with jax.named_scope("forward"):
         blocks_landed(flights[0])
         flights.append(send_blocks(me, fl, out_w.at[2], full_r, sems_w, sems_l.at[2, 0]))
-        c_a = forward(0, send_a, slots_a, sems_a)
+        products(0, send_a)
+        c_a = scatter_x(me, fl, send_a, slots_a, sems_a)
         blocks_landed(flights[1])
-        c_d = forward(1, send_d, slots_d, sems_d)
+        products(1, send_d)
         landed(c_a)
         cross_a = cross(0, send_a, slots_a)
+        c_d = scatter_x(me, fl, send_d, slots_d, sems_d)
     with jax.named_scope("hidden"):
         landed([cross_a])
         gate_pre, up_pre = joined(0, send_a, slots_a, 0), joined(0, send_a, slots_a, 1)
         val, slope, curve = gelu_parts(gate_pre)
         slope_up = slope * up_pre
         hh[0, my_rows, :] = (val * up_pre).astype(BF)
+        c_h0 = gather_x(me, fl, hh.at[0:1], sems_h.at[0])
         mm[0, my_rows, :] = slope_up
         mm[1, my_rows, :] = val
         own[0] = slope
         own[1] = up_pre * curve
         landed(c_d)
         cross_d = cross(1, send_d, slots_d)
-        landed([cross_d])
-        gate_dot, up_dot = joined(1, send_d, slots_d, 0), joined(1, send_d, slots_d, 1)
-        hh[1, my_rows, :] = (mm[0, my_rows, :] * gate_dot + mm[1, my_rows, :] * up_dot).astype(BF)
-        c_h = gather_x(me, fl, hh, sems_h)
-        own[2] = gate_dot
-        own[3] = up_dot
 
     def transposed(i, s):
         for b in range(DB // 128):
@@ -575,8 +571,6 @@
             start_t[i, :, cols] = s[cols, :].astype(F32).T.astype(BF)
 
     with jax.named_scope("starts"):
-        landed(c_h)
-        c_m = gather_x(me, fl, mm, sems_m)
         blocks_landed(flights[2])
         for i in range(NF // 2):
             rows = slice(i * 2 * WR, (i + 1) * 2 * WR)
@@ -594,35 +588,35 @@
     def dot_post(total, rows, lanes):
         return (total / float(TOK)).astype(BF)
 
-    def both(first, second, posts, finals, second_partial):
-        first.cores()
-        second_partial()
-        second.cores()
-        first.ys()
-        second.ys()
-        first.zs()
-        second.zs()
-        first.reduce(finals[0], posts[0])
-        second.reduce(finals[1], posts[1])
-        first.spread()
-        second.spread()
-        first.collect()
-
     ch_o = Chunk(me, fl, acc_o, send_o, (o0, o1, o2, o3, o4, o5), whole_low, 640, whole_back, 512)
     ch_p = Chunk(me, fl, acc_p, send_p, (p0, p1, p2, p3, p4, p5), whole_low, 640, whole_back, 512)
     with jax.named_scope("outputs"):
+        landed(c_h0)
         ch_o.put(nt(hh[0], w_down[...]))
-        both(
-            ch_o,
-            ch_p,
-            (out_post, dot_post),
-            (go, gd),
-            lambda: ch_p.put(nt(hh[1], w_down[...]) + nt(hh[0], s_down[...])),
-        )
+        ch_o.cores()
+        landed([cross_d])
+        gate_dot, up_dot = joined(1, send_d, slots_d, 0), joined(1, send_d, slots_d, 1)
+        hh[1, my_rows, :] = (mm[0, my_rows, :] * gate_dot + mm[1, my_rows, :] * up_dot).astype(BF)
+        c_h1 = gather_x(me, fl, hh.at[1:2], sems_h.at[1])
+        own[2] = gate_dot
+        own[3] = up_dot
+        ch_o.ys()
+        landed(c_h1)
+        c_m = gather_x(me, fl, mm, sems_m)
+        ch_p.put(nt(hh[1], w_down[...]) + nt(hh[0], s_down[...]))
+        ch_p.cores()
+        ch_o.zs()
+        ch_p.ys()
+        ch_o.reduce(go, out_post)
+        ch_p.zs()
+        ch_o.spread()
+        ch_p.reduce(gd, dot_post)
+        ch_o.collect()
     with jax.named_scope("back"):
         partial(send_b, 0, nn(go[...], w_down[...]))
         c_b = scatter_x(me, fl, send_b, slots_b, sems_b)
         c_far = [far(0)]
+        ch_p.spread()
         ch_p.collect()
         partial(send_c, 0, nn(gd[...], w_down[...]) + nn(go[...], s_down[...]))
         c_c = scatter_x(me, fl, send_c, slots_c, sems_c)
@@ -810,7 +804,7 @@
         + [pltpu.VMEM((3, HB, DB), BF), pltpu.VMEM((3, HB, DB), F32)] + [pltpu.VMEM((2, 2, TQ, HB), BF)] * 2
         + [pltpu.VMEM((TOK, TOK), F32), pltpu.VMEM((3, TOK, TOK), F32), pltpu.VMEM((2, TOK, TOK), BF), dma((2, 3))]
         + xround(4) + xround(4)
-        + [pltpu.VMEM((4, TQ, HB), F32), pltpu.VMEM((2, TOK, HB), BF), dma((2, 3)), pltpu.VMEM((2, TOK, HB), F32), dma((2, 3))]
+        + [pltpu.VMEM((4, TQ, HB), F32), pltpu.VMEM((2, TOK, HB), BF), dma((2, 2, 3)), pltpu.VMEM((2, TOK, HB), F32), dma((2, 3))]
         + [pltpu.VMEM((TOK, DB), F32), pltpu.VMEM((TOK, DB), BF)] * 2
         + chunk_scratch(640) + chunk_scratch(640)
         + [pltpu.VMEM((TOK, DB), BF)] * 2

time: 207 us -> 203 us (0.981)
  Pallas kernels: 199 us -> 194 us
    pallas_call x1, Pallas kernels: 199 us -> 194 us  [rounds(): pl.pallas_call(kernel, out_shape=(wide, wide, wide, jax.ShapeDtypeStruct(...]
where the time goes in v5:
time: 203 us; the launch traced here: 202 us
  Pallas kernels  194 us (96%)
  local copies, waits for them, and re-layouts  5.96 us (3%)
  between operations  2.42 us (1%)
    pallas_call x1, Pallas kernels, rounds(): pl.pallas_call(kernel, out_shape=(wide, wide, wide, jax.ShapeDtypeStruct(...  194 us
    unnamed x10, local copies, waits for them, and re-layouts  5.96 us

profile of v5, /device:TPU:1, one launch (start us, length us, event | category | flops | bytes accessed | tf_op | source)
XLA Modules:
  0.0 202.5 jit_solution(1681568208882686534)
XLA Ops:
  0.6 194.1 %arnoldi.1 = (f32[288,1152]{1,0:T(8,128)}, f32[288,1152]{1,0:T(8,128)}, f32[288,1152]{1,0:T(8,128)}, f32[4]{0:T(128)}, f32[1]{0:T(128)}) custom-call(bf16[320,1152]{1,0:T(8,128)(2,1)} %x.1, bf16[320,1152]{1,0:T(8,128)(2,1)} %target.1, bf16[72,4608]{1,0:T(8,128)(2,1)} %in_wg.1, bf16[72,4608]{1,0:T(8,128)(2,1)} %in_wu.1, bf16[72,4608]{1,0:T(8,128)(2,1)} %bitcast.12, ...), custom_call_target="tpu_custom_call" | custom-call | tf_op jit(solution)/shard_map/arnoldi/pallas_call | solution.py:820
  194.7 0.0 copy-start.1
  194.7 2.6 %copy.18 = f32[1152,1,288]{0,2,1:T(8,128)} copy(f32[1152,1,288]{0,2,1:T(8,128)} %bitcast.11) | data formatting | bytes 2654208
  197.3 0.0 copy-done.1
  197.3 0.0 copy-start
  197.3 1.1 copy.19
  198.4 0.7 copy-done
  199.1 0.0 copy-start.2
  199.1 1.1 copy.20
  200.2 0.0 copy-done.2
  200.2 0.5 copy.21
Async XLA Ops:
  194.7 2.6 %copy-start.1 = (f32[288,1152]{1,0:T(8,128)S(1)}, f32[288,1152]{1,0:T(8,128)}, u32[]{:S(2)}) copy-start(f32[288,1152]{1,0:T(8,128)} %get-tuple-element.11) | copy-start | bytes 3981316
  197.3 1.8 copy-start
  199.1 1.1 copy-start.2

commit v6 on v5

--- a/solution.py
+++ b/solution.py
@@ -471,7 +471,7 @@
     send_a, slots_a, sems_a, send_d, slots_d, sems_d,
     own, hh, sems_h, mm, sems_m,
     acc_o, send_o, acc_p, send_p,
-    o0, o1, o2, o3, o4, o5, p0, p1, p2, p3, p4, p5,
+    o0, o1, o2, o3, o4, o5, p0, p1, p2, p3, p4, p5, s0, s1, s2, s3, s4, s5,
     go, gd,
     send_b, slots_b, sems_b, send_c, slots_c, sems_c,
     gu1, sems_g1, u1d, tan2, h2,
@@ -589,7 +589,8 @@
         return (total / float(TOK)).astype(BF)
 
     ch_o = Chunk(me, fl, acc_o, send_o, (o0, o1, o2, o3, o4, o5), whole_low, 640, whole_back, 512)
-    ch_p = Chunk(me, fl, acc_p, send_p, (p0, p1, p2, p3, p4, p5), whole_low, 640, whole_back, 512)
+    ch_p = Chunk(me, fl, acc_p, send_p, (p0, p1, p2, p3, p4, p5), outer_low, 384, outer_low, 384)
+    ch_s = Chunk(me, fl, acc_p, send_p, (s0, s1, s2, s3, s4, s5), inner_low, 256, inner_back, 128)
     with jax.named_scope("outputs"):
         landed(c_h0)
         ch_o.put(nt(hh[0], w_down[...]))
@@ -605,19 +606,25 @@
         c_m = gather_x(me, fl, mm, sems_m)
         ch_p.put(nt(hh[1], w_down[...]) + nt(hh[0], s_down[...]))
         ch_p.cores()
+        ch_s.cores()
         ch_o.zs()
         ch_p.ys()
+        ch_s.ys()
         ch_o.reduce(go, out_post)
         ch_p.zs()
+        ch_s.zs()
         ch_o.spread()
         ch_p.reduce(gd, dot_post)
+        ch_s.reduce(gd, dot_post)
         ch_o.collect()
     with jax.named_scope("back"):
         partial(send_b, 0, nn(go[...], w_down[...]))
         c_b = scatter_x(me, fl, send_b, slots_b, sems_b)
         c_far = [far(0)]
         ch_p.spread()
+        ch_s.spread()
         ch_p.collect()
+        ch_s.collect()
         partial(send_c, 0, nn(gd[...], w_down[...]) + nn(go[...], s_down[...]))
         c_c = scatter_x(me, fl, send_c, slots_c, sems_c)
         image = tn(hh[1], go[...]) + tn(hh[0], gd[...])
@@ -787,7 +794,7 @@
 
     for copy in fl.sent:
         copy.wait_send()
-    for chunk in (ch_o, ch_p, ch_q, ch_r):
+    for chunk in (ch_o, ch_p, ch_s, ch_q, ch_r):
         chunk.drain()
 
 
@@ -806,7 +813,7 @@
         + xround(4) + xround(4)
         + [pltpu.VMEM((4, TQ, HB), F32), pltpu.VMEM((2, TOK, HB), BF), dma((2, 2, 3)), pltpu.VMEM((2, TOK, HB), F32), dma((2, 3))]
         + [pltpu.VMEM((TOK, DB), F32), pltpu.VMEM((TOK, DB), BF)] * 2
-        + chunk_scratch(640) + chunk_scratch(640)
+        + chunk_scratch(640) + chunk_scratch(384) + chunk_scratch(256)
         + [pltpu.VMEM((TOK, DB), BF)] * 2
         + xround(1) + xround(1)
         + [pltpu.VMEM((2, TOK, HB), BF), dma((2, 3)), pltpu.VMEM((HB, DB), BF), pltpu.VMEM((2, TOK, HB), F32), pltpu.VMEM((TOK, HB), BF)]

time: 203 us -> 204 us (level)
  no operation moved by 1% of the time
where the time goes in v6:
time: 204 us
  Pallas kernels  195 us (96%)
  local copies, waits for them, and re-layouts  5.96 us (3%)
  between operations  2.42 us (1%)
    pallas_call x1, Pallas kernels, rounds(): pl.pallas_call(kernel, out_shape=(wide, wide, wide, jax.ShapeDtypeStruct(...  195 us
    unnamed x10, local copies, waits for them, and re-layouts  5.96 us

profile of v6, /device:TPU:1, one launch (start us, length us, event | category | flops | bytes accessed | tf_op | source)
XLA Modules:
  0.0 203.7 jit_solution(18113616296536861157)
XLA Ops:
  0.6 195.4 %arnoldi.1 = (f32[288,1152]{1,0:T(8,128)}, f32[288,1152]{1,0:T(8,128)}, f32[288,1152]{1,0:T(8,128)}, f32[4]{0:T(128)}, f32[1]{0:T(128)}) custom-call(bf16[320,1152]{1,0:T(8,128)(2,1)} %x.1, bf16[320,1152]{1,0:T(8,128)(2,1)} %target.1, bf16[72,4608]{1,0:T(8,128)(2,1)} %in_wg.1, bf16[72,4608]{1,0:T(8,128)(2,1)} %in_wu.1, bf16[72,4608]{1,0:T(8,128)(2,1)} %bitcast.12, ...), custom_call_target="tpu_custom_call" | custom-call | tf_op jit(solution)/shard_map/arnoldi/pallas_call | solution.py:827
  196.0 0.0 copy-start.1
  196.0 2.6 %copy.18 = f32[1152,1,288]{0,2,1:T(8,128)} copy(f32[1152,1,288]{0,2,1:T(8,128)} %bitcast.11) | data formatting | bytes 2654208
  198.6 0.0 copy-done.1
  198.6 0.0 copy-start
  198.6 1.1 copy.19
  199.6 0.7 copy-done
  200.4 0.0 copy-start.2
  200.4 1.1 copy.20
  201.4 0.0 copy-done.2
  201.4 0.5 copy.21
Async XLA Ops:
  196.0 2.6 %copy-start.1 = (f32[288,1152]{1,0:T(8,128)S(1)}, f32[288,1152]{1,0:T(8,128)}, u32[]{:S(2)}) copy-start(f32[288,1152]{1,0:T(8,128)} %get-tuple-element.11) | copy-start | bytes 3981316
  198.6 1.8 copy-start
  200.4 1.1 copy-start.2
